TPU v7x, 32 devices: a whole 2x2x4 slice. The times are simulated.
32 devices in a mesh: group: 8 (over z, x), narrow: 4 (over y, core).
Axes of the slice: x: 2, y: 2, z: 4, core: 2. Of those that a mesh axis runs over, the one named last changes fastest.
Arguments:
- series_values: float32 [128, 1024], P(('group', 'narrow')), may hold values from -60 to 60, as said below
- observed: int32 [128, 1024], P(('group', 'narrow')), may hold values 0 or 1
- lag_steps: int32 [84], replicated, may hold values from 1 to 511
- lag_flags: int32 [84], replicated, may hold values 0 or 1
- dataset_ids: int32 [128], P(('group', 'narrow')), may hold values from 0 to 3
- in_proj: float32 [86, 144], replicated, may hold values from -0.625 to 0.625
- gain_attn: float32 [144], replicated, may hold values from 0.5 to 1.5
- query_proj: float32 [144, 144], replicated, may hold values from -0.5 to 0.5
- key_proj: float32 [144, 144], replicated, may hold values from -0.5 to 0.5
- value_proj: float32 [144, 144], replicated, may hold values from -0.5 to 0.5
- out_proj: float32 [144, 144], replicated, may hold values from -1 to 1
- gain_ffn: float32 [144], replicated, may hold values from 0.5 to 1.5
- gate_proj: float32 [144, 384], replicated, may hold values from -0.5 to 0.5
- up_proj: float32 [144, 384], replicated, may hold values from -0.5 to 0.5
- down_proj: float32 [384, 144], replicated, may hold values from -0.625 to 0.625
- cotangent: float32 [128, 1024, 144], P(('group', 'narrow')), may hold values from -6 to 6
Outputs:
- activations: float32 [128, 1024, 144], P(('group', 'narrow'))
- input_grad: float32 [128, 1024, 144], P(('group', 'narrow'))
- grad_in_proj: float32 [86, 144], P(None, 'narrow')
- grad_gain_attn: float32 [144], P('narrow')
- grad_query_proj: float32 [144, 144], P('narrow')
- grad_key_proj: float32 [144, 144], P('narrow')
- grad_value_proj: float32 [144, 144], P('narrow')
- grad_out_proj: float32 [144, 144], P('narrow')
- grad_gain_ffn: float32 [144], P('narrow')
- grad_gate_proj: float32 [144, 384], P(None, 'narrow')
- grad_up_proj: float32 [144, 384], P(None, 'narrow')
- grad_down_proj: float32 [384, 144], P('narrow')
Inputs may be any that keep to these rules, and one draw needn't show every extreme that they name: `series_values`: raw series values; each series has its own magnitude.
All inputs are finite; a program needn't handle non-finite values. No bound on the sum of `observed` on one device may be relied on, other than what follows from the above.
Results may differ from a plain program's by a relative error of at most 0.0003.
Values sent between devices are 32-bit elements; how exact they have to be, the bound alone decides.
A program may use at most 640 MiB of HBM per device.

v0:
```python
import functools

import jax
import jax.numpy as jnp
import numpy as np
from jax import lax
from jax.experimental import pallas as pl
from jax.experimental.pallas import tpu as pltpu
from jax.sharding import PartitionSpec as P

HEADS = 9
HD = 16
DSETS = 4
FPAD = 96
QB = 256
TA = 512
TC = 256
TD = 256
NLAG = 84

NORM_EPS = 1e-05
SCALE_EPS = 1e-05
LOG2E = 1.4426950408889634
LN2 = 0.6931471805599453

F32 = jnp.float32
BF16 = jnp.bfloat16


def nn(left, right):
    return lax.dot_general(left, right, (((1,), (0,)), ((), ())), preferred_element_type=F32)


def nt(left, right):
    return lax.dot_general(left, right, (((1,), (1,)), ((), ())), preferred_element_type=F32)


def split(x):
    hi = x.astype(BF16)
    return hi, (x - hi.astype(F32)).astype(BF16)


def split3(x):
    hi = x.astype(BF16)
    rest = x - hi.astype(F32)
    mid = rest.astype(BF16)
    return hi, mid, (rest - mid.astype(F32)).astype(BF16)


def cat3(x):
    hi, lo = split(x)
    return jnp.concatenate([hi, hi, lo], axis=0)


def weight_cat(w):
    hi, lo = split(w)
    hi, lo = hi.astype(F32), lo.astype(F32)
    return jnp.concatenate([hi, lo, hi], axis=0).T.astype(BF16)


def weight_stack(w):
    hi, lo = split(w)
    return jnp.concatenate([hi, lo], axis=0)


def mm_stack(stack, x):
    m = stack.shape[0] // 2
    hi, lo = split(x)
    both = nn(stack, hi)
    return both[:m] + both[m:] + nn(stack[:m], lo)


def outer_sum(left, right):
    m = left.shape[0]
    lh, ll = split(left)
    rh, rl = split(right)
    both = nt(jnp.concatenate([lh, ll], axis=0), rh)
    return both[:m] + both[m:] + nt(lh, rl)


def column(row):
    n = row.shape[0]
    return jnp.broadcast_to(row[None, :], (8, n)).T[:, :1]


def lane_fold(x):
    total = x[:, :128]
    for i in range(1, x.shape[1] // 128):
        total = total + x[:, i * 128 : (i + 1) * 128]
    return total


def rotate(x, cos, sin):
    t = x.shape[1]
    pairs = x.reshape(HEADS, 2, HD // 2, t)
    a, b = pairs[:, 0], pairs[:, 1]
    first = a * cos - b * sin
    second = a * sin + b * cos
    return jnp.stack([first, second], axis=1).reshape(HEADS * HD, t)


def row_scales(scale, nlag):
    row = lax.broadcasted_iota(jnp.int32, (FPAD, 128), 0)
    scales = jnp.full((FPAD, 128), scale, F32)
    inverse, logs = 1.0 / scales, jnp.log(scales)
    return jnp.where(row < nlag, inverse, jnp.where(row == nlag, logs, 1.0))[:, :1]


def prepare_kernel(
    lag_ref, flag_ref, vals_ref, obs_ref, in_ref, wq_ref, wk_ref, wv_ref, wo_ref, wg_ref, wu_ref, wd_ref, ga_ref, gf_ref,
    feat_ref, w_in, w_qkv, w_out, w_gu, w_down, w_dh, w_dgu, w_dm, w_dqkv, gains,
):
    n_series, t = vals_ref.shape
    d, nf = in_ref.shape
    nlag = lag_ref.shape[0]
    ff = wg_ref.shape[1]
    obs = obs_ref[...].astype(F32)
    both = jnp.concatenate([vals_ref[...] * obs, obs], axis=0)
    lanes = lax.broadcasted_iota(jnp.int32, both.shape, 1)

    def one_lag(j, missing):
        lag = lag_ref[j]
        moved = jnp.where(lanes >= lag, pltpu.roll(both, lag, 1), 0.0)
        for s in range(n_series):
            feat_ref[s, pl.ds(j, 1), :] = moved[s : s + 1]
        return missing + flag_ref[j].astype(F32) * (1.0 - moved[n_series:])

    missing = lax.fori_loop(0, nlag, one_lag, jnp.zeros((n_series, t), F32), unroll=4)
    for s in range(n_series):
        feat_ref[s, nlag : nlag + 1, :] = jnp.ones((1, t), F32)
        feat_ref[s, nlag + 1 : nlag + 2, :] = missing[s : s + 1] * nlag**-0.5
        feat_ref[s, nlag + 2 :, :] = jnp.zeros((FPAD - nlag - 2, t), F32)

    w_in_rows = jnp.concatenate([in_ref[...].T, jnp.zeros((FPAD - nf, d), F32)], axis=0)
    w_in[...] = weight_cat(w_in_rows)
    for i, ref in enumerate((wq_ref, wk_ref, wv_ref)):
        w_qkv[i * d : (i + 1) * d, :] = weight_cat(ref[...])
        w_dqkv[:, i * d : (i + 1) * d] = weight_stack(ref[...])
    w_out[...] = weight_cat(wo_ref[...])
    w_gu[:ff, :] = weight_cat(wg_ref[...])
    w_gu[ff:, :] = weight_cat(wu_ref[...])
    w_down[...] = weight_stack(wd_ref[...])
    w_dh[...] = weight_cat(wd_ref[...])
    w_dgu[:, :ff] = weight_stack(wg_ref[...])
    w_dgu[:, ff:] = weight_stack(wu_ref[...])
    w_dm[...] = weight_cat(wo_ref[...].T)
    gains[...] = jnp.zeros_like(gains)
    gains[:, :1] = column(ga_ref[...])
    gains[:, 1:2] = column(gf_ref[...])


def forward_kernel(
    scale_ref, feat_ref, w_in, w_qkv, w_out, w_gu, w_down, w_dh, w_dgu, w_dm, gains, cos_ref, sin_ref, cot_ref,
    act_ref, q_ref, k_ref, v_ref, dm_ref, st_ref, da_ref, x_ref, b1_ref,
    mixed_ref, g_gu, g_down, g_out, g_gf,
):
    step = pl.program_id(0)
    d, t = cot_ref.shape[1], cot_ref.shape[2]
    ff = w_dh.shape[0]
    gain_attn, gain_ffn = gains[:, :1], gains[:, 1:2]
    scales = row_scales(scale_ref[step], NLAG)

    @pl.when(step == 0)
    def _():
        for ref in (g_gu, g_down, g_out, g_gf):
            ref[...] = jnp.zeros_like(ref)

    st_ref[0] = jnp.zeros(st_ref.shape[1:], F32)

    def project(i, _):
        cols = pl.ds(pl.multiple_of(i * TA, TA), TA)
        x = nn(w_in[...], cat3(feat_ref[0, :, cols] * scales))
        x_ref[0, :, cols] = x
        normed = x * lax.rsqrt(jnp.mean(x * x, axis=0, keepdims=True) + NORM_EPS) * gain_attn
        qkv = nn(w_qkv[...], cat3(normed))
        cos, sin = cos_ref[:, cols], sin_ref[:, cols]
        q_ref[0, :, cols] = rotate(qkv[:d], cos, sin) * (HD**-0.5 * LOG2E)
        k_ref[0, :, cols] = rotate(qkv[d : 2 * d], cos, sin)
        v_ref[0, :, cols] = qkv[2 * d :]
        return 0

    lax.fori_loop(0, t // TA, project, 0)

    causal = lax.broadcasted_iota(jnp.int32, (QB, QB), 0) <= lax.broadcasted_iota(jnp.int32, (QB, QB), 1)

    def head(h, _):
        rows = pl.ds(pl.multiple_of(h * HD, HD), HD)
        qh, ql = split(q_ref[0, rows, :])
        qc = jnp.concatenate([qh, ql, qh], axis=0)
        kh, kl = split(k_ref[0, rows, :])
        kh, kl = kh.astype(F32), kl.astype(F32)
        kc = jnp.concatenate([kh, kh, kl], axis=0).T.astype(BF16)
        vh, vl = split(v_ref[0, rows, :])
        vs = jnp.concatenate([vh, vl], axis=0)
        for block in range(t // QB):
            lo, top = block * QB, (block + 1) * QB
            s = nn(kc[:top], qc[:, lo:top])
            last = jnp.where(causal, s[lo:], -1e30)
            s = jnp.concatenate([s[:lo], last], axis=0) if block else last
            m = jnp.max(s, axis=0, keepdims=True)
            p = jnp.exp2(s - m)
            total = jnp.sum(p, axis=0, keepdims=True)
            ph, pl_ = split(p)
            both = nn(vs[:, :top], ph)
            out = both[:HD] + both[HD:] + nn(vh[:, :top], pl_)
            mixed_ref[rows, lo:top] = out / total
            st_ref[0, pl.ds(h, 1), lo:top] = m + jnp.log2(total)
        return 0

    lax.fori_loop(0, HEADS, head, 0, unroll=3)

    def feed(i, _):
        cols = pl.ds(pl.multiple_of(i * TC, TC), TC)
        mixed = mixed_ref[:, cols]
        attended = x_ref[0, :, cols] + nn(w_out[...], cat3(mixed))
        r2 = lax.rsqrt(jnp.mean(attended * attended, axis=0, keepdims=True) + NORM_EPS)
        scaled = attended * r2
        normed2 = scaled * gain_ffn
        gu = nn(w_gu[...], cat3(normed2))
        gate, up = gu[:ff], gu[ff:]
        sig = 1.0 / (1.0 + jnp.exp(-gate))
        silu = gate * sig
        hidden = silu * up
        act_ref[0, :, cols] = attended + mm_stack(w_down[...], hidden)

        g = cot_ref[0, :, cols]
        dh = nn(w_dh[...], cat3(g))
        dgate = dh * up * (sig + silu * (1.0 - sig))
        dup = dh * silu
        dgu = jnp.concatenate([dgate, dup], axis=0)
        dn2 = mm_stack(w_dgu[...], dgu)
        g_down[...] += outer_sum(hidden, g)
        g_gu[...] += outer_sum(dgu, normed2)
        weighted = dn2 * gain_ffn
        inner = jnp.mean(weighted * attended, axis=0, keepdims=True)
        da = g + r2 * weighted - attended * (r2 * r2 * r2 * inner)
        da_ref[0, :, cols] = da
        g_gf[...] += lane_fold(dn2 * scaled)
        g_out[...] += outer_sum(mixed, da)
        dm = nn(w_dm[...], cat3(da))
        dm_ref[0, :, cols] = dm
        prod = (dm * mixed).reshape(HEADS, HD, TC)
        for h in range(HEADS):
            st_ref[0, 16 + h : 17 + h, cols] = jnp.sum(prod[h], axis=0, keepdims=True)
        return 0

    lax.fori_loop(0, t // TC, feed, 0)

    @pl.when(step == pl.num_programs(0) - 1)
    def _():
        parts = b1_ref.shape[0]
        fs, ds = ff // parts, d // parts
        g_gu_t = g_gu[...].T
        g_down_t = g_down[...].T
        g_out_t = g_out[...].T
        gf = jnp.sum(g_gf[...], axis=1, keepdims=True)
        b1_ref[...] = jnp.zeros_like(b1_ref)
        for n in range(parts):
            gf_own = jnp.concatenate([gf[n * ds : (n + 1) * ds], jnp.zeros((d - ds, 1), F32)], axis=0)
            share = jnp.concatenate([
                g_gu_t[:, n * fs : (n + 1) * fs], g_gu_t[:, ff + n * fs : ff + (n + 1) * fs],
                g_down_t[:, n * fs : (n + 1) * fs], g_out_t[:, n * ds : (n + 1) * ds], gf_own,
            ], axis=1)
            put_share(b1_ref, n, share)


def put_share(ref, n, share):
    rows, cols = share.shape
    pad_rows, pad_cols = -rows % 8, -cols % 128
    if pad_rows:
        share = jnp.concatenate([share, jnp.zeros((pad_rows, cols), F32)], axis=0)
    if pad_cols:
        share = jnp.concatenate([share, jnp.zeros((share.shape[0], pad_cols), F32)], axis=1)
    height = share.shape[0]
    for c in range(share.shape[1] // 128):
        ref[n, c * height : (c + 1) * height, :] = share[:, c * 128 : (c + 1) * 128]


def backward_kernel(
    scale_ref, q_ref, k_ref, v_ref, dm_ref, st_ref, da_ref, x_ref, feat_ref, w_dqkv, gains, cos_ref, sin_ref,
    dx_ref, b2_ref,
    dqkv_ref, g_qkv, g_in, g_ga,
):
    step = pl.program_id(0)
    d, t = q_ref.shape[1], q_ref.shape[2]

    @pl.when(step == 0)
    def _():
        for ref in (g_qkv, g_in, g_ga):
            ref[...] = jnp.zeros_like(ref)

    nb = t // QB
    causal = lax.broadcasted_iota(jnp.int32, (QB, QB), 0) >= lax.broadcasted_iota(jnp.int32, (QB, QB), 1)
    ones = (lax.broadcasted_iota(jnp.int32, (HD, t), 0) < 3).astype(BF16)

    def extras(row):
        a, b, c = split3(row)
        pieces = jnp.concatenate([a.astype(F32), b.astype(F32), c.astype(F32)], axis=0)
        return jnp.concatenate([pieces, jnp.zeros((HD - 3, t), F32)], axis=0)

    def sides(block, row):
        hi, lo = split(block)
        hf, lf = hi.astype(F32), lo.astype(F32)
        tall = jnp.concatenate([hf, lf, hf, extras(-row)], axis=0).T.astype(BF16)
        return tall, jnp.concatenate([hi, lo], axis=0), hi

    def head(h, _):
        def rows_at(first):
            return pl.ds(pl.multiple_of(first + h * HD, HD), HD)

        rows = rows_at(0)
        qc, qs, qh = sides(q_ref[0, rows, :], st_ref[0, pl.ds(h, 1), :])
        mc, ms, mh = sides(dm_ref[0, rows, :], st_ref[0, pl.ds(16 + h, 1), :])
        kh, kl = split(k_ref[0, rows, :])
        kc = jnp.concatenate([kh, kh, kl, ones], axis=0)
        ks = jnp.concatenate([kh, kl], axis=0)
        vh, vl = split(v_ref[0, rows, :])
        vc = jnp.concatenate([vh, vh, vl, ones], axis=0)

        def scores(block):
            lo = block * QB
            cols = slice(lo, lo + QB)
            return nn(qc[lo:], kc[:, cols]), nn(mc[lo:], vc[:, cols])

        dq_blocks = [None] * nb
        ahead = scores(0)
        for block in range(nb):
            lo = block * QB
            cols = slice(lo, lo + QB)
            s, dp = ahead
            if block + 1 < nb:
                ahead = scores(block + 1)
            p = jnp.exp2(s)
            first = jnp.where(causal, p[:QB], 0.0)
            p = jnp.concatenate([first, p[QB:]], axis=0) if block + 1 < nb else first
            ds = p * dp
            ph, pl_ = split(p)
            dh, dl = split(ds)
            both = nn(ms[:, lo:], ph)
            dqkv_ref[rows_at(2 * d), cols] = both[:HD] + both[HD:] + nn(mh[:, lo:], pl_)
            both = nn(qs[:, lo:], dh)
            dqkv_ref[rows_at(d), cols] = both[:HD] + both[HD:] + nn(qh[:, lo:], dl)
            th, tl = split(ds.T)
            both = nn(ks[:, cols], th)
            part = both[:HD] + both[HD:] + nn(kh[:, cols], tl)
            for i in range(block, nb):
                piece = part[:, (i - block) * QB : (i - block + 1) * QB]
                dq_blocks[i] = piece if dq_blocks[i] is None else dq_blocks[i] + piece
        for i in range(nb):
            dqkv_ref[rows, i * QB : (i + 1) * QB] = dq_blocks[i]
        return 0

    lax.fori_loop(0, HEADS, head, 0, unroll=3)

    gain = gains[:, :1]
    scales = row_scales(scale_ref[step], NLAG)

    def finish(i, _):
        cols = pl.ds(pl.multiple_of(i * TD, TD), TD)
        cos, sin = cos_ref[:, cols], -sin_ref[:, cols]
        dq = rotate(dqkv_ref[:d, cols], cos, sin) * HD**-0.5
        dk = rotate(dqkv_ref[d : 2 * d, cols], cos, sin) * LN2
        dqkv = jnp.concatenate([dq, dk, dqkv_ref[2 * d :, cols]], axis=0)
        x = x_ref[0, :, cols]
        r = lax.rsqrt(jnp.mean(x * x, axis=0, keepdims=True) + NORM_EPS)
        xr = x * r
        dn = mm_stack(w_dqkv[...], dqkv)
        g_qkv[...] += outer_sum(dqkv, xr * gain)
        weighted = dn * gain
        inner = jnp.mean(weighted * x, axis=0, keepdims=True)
        dx = da_ref[0, :, cols] + r * weighted - x * (r * r * r * inner)
        dx_ref[0, :, cols] = dx
        g_ga[...] += lane_fold(dn * xr)
        g_in[...] += outer_sum(dx, feat_ref[0, :, cols] * scales)
        return 0

    lax.fori_loop(0, t // TD, finish, 0)

    @pl.when(step == pl.num_programs(0) - 1)
    def _():
        parts = b2_ref.shape[0]
        ds = d // parts
        g_qkv_t = g_qkv[...].T
        ga = jnp.sum(g_ga[...], axis=1, keepdims=True)
        b2_ref[...] = jnp.zeros_like(b2_ref)
        for n in range(parts):
            own = slice(n * ds, (n + 1) * ds)
            put_share(b2_ref, n, jnp.concatenate([g_qkv_t[own], g_in[own, :], ga[own]], axis=1))


def reduce_kernel(b1_ref, b2_ref, out_ref, recv1, pair, recv2, share, recv3, sem_s, sem_r, gsem_s, gsem_r, hsem_s, hsem_r):
    ny = b1_ref.shape[0]
    r1, r2 = b1_ref.shape[2], b2_ref.shape[2]
    groups, chunk = recv3.shape[0], recv3.shape[1]
    g = lax.axis_index("group")
    n = lax.axis_index("narrow")
    core, y = lax.rem(n, 2), lax.div(n, 2)
    other = 1 - core

    def at(group, narrow):
        return (group, narrow)

    mesh_id = pl.DeviceIdType.MESH
    barrier = pltpu.get_barrier_semaphore()
    pl.semaphore_signal(barrier, inc=1, device_id=at(g, y * 2 + other), device_id_type=mesh_id)
    for off in range(1, ny):
        peer = lax.rem(y + off, ny)
        pl.semaphore_signal(barrier, inc=1, device_id=at(g, peer * 2 + core), device_id_type=mesh_id)
    for off in range(1, groups):
        pl.semaphore_signal(barrier, inc=1, device_id=at(lax.rem(g + off, groups), n), device_id_type=mesh_id)
    pl.semaphore_wait(barrier, 1 + (ny - 1) + (groups - 1))

    def copy(src, dst, send, recv, to):
        return pltpu.make_async_remote_copy(
            src_ref=src, dst_ref=dst, send_sem=send, recv_sem=recv, device_id=to, device_id_type=mesh_id
        )

    sibling = at(g, y * 2 + other)
    first = copy(b1_ref.at[:, other], recv1.at[:, pl.ds(0, r1)], sem_s.at[0], sem_r.at[0], sibling)
    second = copy(b2_ref.at[:, other], recv1.at[:, pl.ds(r1, r2)], sem_s.at[1], sem_r.at[1], sibling)
    first.start()
    second.start()
    first.wait_recv()
    second.wait_recv()
    for i in range(ny):
        pair[i, :r1] = b1_ref[i, core] + recv1[i, :r1]
        pair[i, r1 : r1 + r2] = b2_ref[i, core] + recv1[i, r1 : r1 + r2]

    sends = []
    for off in range(1, ny):
        peer = lax.rem(y + off, ny)
        sends.append(copy(pair.at[peer], recv2.at[off - 1], gsem_s.at[off], gsem_r.at[off], at(g, peer * 2 + core)))
        sends[-1].start()
    for s in sends:
        s.wait_recv()
    total = pair[y]
    for off in range(1, ny):
        total += recv2[off - 1]
    share[...] = total.reshape(share.shape)

    sends_b = []
    for off in range(1, groups):
        peer = lax.rem(g + off, groups)
        sends_b.append(copy(share.at[peer], recv3.at[off], hsem_s.at[0, off], hsem_r.at[0, off], at(peer, n)))
        sends_b[-1].start()
    recv3[0] = share[g]
    for s in sends_b:
        s.wait_recv()
    out_ref[g] = jnp.sum(recv3[...], axis=0)
    sends_c = []
    for off in range(1, groups):
        peer = lax.rem(g + off, groups)
        sends_c.append(copy(out_ref.at[g], out_ref.at[g], hsem_s.at[1, off], hsem_r.at[1, off], at(peer, n)))
        sends_c[-1].start()
    for s in sends_c:
        s.wait_recv()
    for s in [first, second] + sends + sends_b + sends_c:
        s.wait_send()


def unpack_kernel(
    total_ref, g_in, g_ga, g_q, g_k, g_v, g_out, g_gf, g_gate, g_up, g_down,
):
    d, fs = g_gate.shape
    ds, nf = g_in.shape
    wide = round_up(3 * fs + ds + 1, 128) // 128
    one = jnp.concatenate([total_ref[c * d : (c + 1) * d, :] for c in range(wide)], axis=1)
    g_gate[...] = one[:, :fs]
    g_up[...] = one[:, fs : 2 * fs]
    g_down[...] = one[:, 2 * fs : 3 * fs]
    g_out[...] = one[:, 3 * fs : 3 * fs + ds].T
    g_gf[...] = one[:ds, 3 * fs + ds]
    base = wide * d
    height = round_up(ds, 8)
    wide = round_up(3 * d + FPAD + 1, 128) // 128
    two = jnp.concatenate([total_ref[base + c * height : base + c * height + ds, :] for c in range(wide)], axis=1)
    g_q[...] = two[:, :d]
    g_k[...] = two[:, d : 2 * d]
    g_v[...] = two[:, 2 * d : 3 * d]
    g_in[...] = two[:, 3 * d : 3 * d + nf]
    g_ga[...] = two[:, 3 * d + FPAD]


def rotation_tables(t):
    freqs = 10000.0 ** (-np.arange(HD // 2, dtype=np.float64) * 2.0 / HD)
    angles = freqs[:, None] * np.arange(t, dtype=np.float64)[None, :]
    return np.cos(angles).astype(np.float32), np.sin(angles).astype(np.float32)


def round_up(n, m):
    return (n + m - 1) // m * m


def on_device(
    groups, parts, series_values, observed, lag_steps, lag_flags, dataset_ids, in_proj, gain_attn, query_proj, key_proj,
    value_proj, out_proj, gain_ffn, gate_proj, up_proj, down_proj, cotangent,
):
    n_series, t = series_values.shape
    nf, d = in_proj.shape
    ff = gate_proj.shape[1]
    fs, ds = ff // parts, d // parts
    onehot, sums = local_sums(series_values, observed, dataset_ids)
    others = exchange_sums(sums, parts)

    cos, sin = rotation_tables(t)
    cos, sin = jnp.asarray(cos), jnp.asarray(sin)
    smem = pl.BlockSpec(memory_space=pltpu.SMEM)
    vmem = pl.BlockSpec(memory_space=pltpu.VMEM)

    def whole(a):
        return pl.BlockSpec(a.shape, lambda i: (0,) * a.ndim)

    def each(rows):
        return pl.BlockSpec((1, rows, t), lambda i: (i, 0, 0))

    def shape(*dims, dtype=F32):
        return jax.ShapeDtypeStruct(dims, dtype)

    params = pltpu.CompilerParams(dimension_semantics=("arbitrary",), vmem_limit_bytes=62 * 2**20)
    plain = pltpu.CompilerParams(vmem_limit_bytes=62 * 2**20)
    in_t, down_t = in_proj.T, down_proj.T
    raw, w_in, w_qkv, w_out, w_gu, w_down, w_dh, w_dgu, w_dm, w_dqkv, gains = pl.pallas_call(
        prepare_kernel,
        in_specs=[smem] * 2 + [vmem] * 12,
        out_specs=[vmem] * 11,
        out_shape=[
            shape(n_series, FPAD, t),
            shape(d, 3 * FPAD, dtype=BF16),
            shape(3 * d, 3 * d, dtype=BF16),
            shape(d, 3 * d, dtype=BF16),
            shape(2 * ff, 3 * d, dtype=BF16),
            shape(2 * d, ff, dtype=BF16),
            shape(ff, 3 * d, dtype=BF16),
            shape(2 * d, 2 * ff, dtype=BF16),
            shape(d, 3 * d, dtype=BF16),
            shape(2 * d, 3 * d, dtype=BF16),
            shape(d, 128),
        ],
        compiler_params=plain,
        cost_estimate=pl.CostEstimate(flops=2 * 10**7, bytes_accessed=8 * 10**6, transcendentals=0),
        name="split_weights_and_shift_lags",
    )(lag_steps, lag_flags, series_values, observed, in_t, query_proj, key_proj, value_proj, out_proj, gate_proj, up_proj,
      down_t, gain_attn, gain_ffn)

    sums = functools.reduce(jnp.add, others, sums)
    set_scale = sums[0] / jnp.maximum(sums[1], 1.0) + SCALE_EPS
    series_scale = jnp.sum(onehot * set_scale[None, :], axis=1)

    rows1 = round_up(3 * fs + ds + 1, 128) // 128 * d
    rows2 = round_up(3 * d + FPAD + 1, 128) // 128 * round_up(ds, 8)
    rows2 = round_up(rows1 + rows2, 8 * groups) - rows1
    full = [w_in, w_qkv, w_out, w_gu, w_down, w_dh, w_dgu, w_dm, gains, cos, sin]
    b1 = shape(parts, rows1, 128)
    act, q, k, v, dm, st, da, x, b1 = pl.pallas_call(
        forward_kernel,
        grid=(n_series,),
        in_specs=[smem, each(FPAD)] + [whole(a) for a in full] + [each(d)],
        out_specs=[each(d)] * 5 + [each(32)] + [each(d)] * 2 + [whole(b1)],
        out_shape=[shape(n_series, d, t)] * 5 + [shape(n_series, 32, t)] + [shape(n_series, d, t)] * 2 + [b1],
        scratch_shapes=[
            pltpu.VMEM((d, t), F32),
            pltpu.VMEM((2 * ff, d), F32),
            pltpu.VMEM((ff, d), F32),
            pltpu.VMEM((d, d), F32),
            pltpu.VMEM((d, 128), F32),
        ],
        compiler_params=params,
        name="forward_and_ffn",
    )(series_scale, raw, *full, jnp.transpose(cotangent, (0, 2, 1)))

    b2 = shape(parts, rows2, 128)
    full = [w_dqkv, gains, cos, sin]
    dx, b2 = pl.pallas_call(
        backward_kernel,
        grid=(n_series,),
        in_specs=[smem] + [each(d)] * 4 + [each(32)] + [each(d)] * 2 + [each(FPAD)] + [whole(a) for a in full],
        out_specs=[each(d), whole(b2)],
        out_shape=[shape(n_series, d, t), b2],
        scratch_shapes=[
            pltpu.VMEM((3 * d, t), F32),
            pltpu.VMEM((3 * d, d), F32),
            pltpu.VMEM((d, FPAD), F32),
            pltpu.VMEM((d, 128), F32),
        ],
        compiler_params=params,
        name="attention_backward",
    )(series_scale, q, k, v, dm, st, da, x, raw, *full)

    total = reduce_grads(b1, b2, groups, parts)
    grads = pl.pallas_call(
        unpack_kernel,
        in_specs=[vmem],
        out_specs=[vmem] * 10,
        out_shape=[
            shape(ds, nf), shape(ds), shape(ds, d), shape(ds, d), shape(ds, d), shape(ds, d), shape(ds),
            shape(d, fs), shape(d, fs), shape(d, fs),
        ],
        compiler_params=plain,
        name="unpack_gradients",
    )(total)
    return (
        jnp.transpose(act, (0, 2, 1)),
        jnp.transpose(dx, (0, 2, 1)),
        grads[0].T,
        *grads[1:9],
        grads[9].T,
    )


def local_sums(series_values, observed, dataset_ids):
    observed_f = observed.astype(F32)
    magnitude = jnp.sum(jnp.abs(series_values) * observed_f, axis=1)
    counted = jnp.sum(observed_f, axis=1)
    onehot = (dataset_ids[:, None] == jnp.arange(DSETS)[None, :]).astype(F32)
    return onehot, jnp.sum(onehot[None] * jnp.stack([magnitude, counted])[:, :, None], axis=1)


def exchange_sums(sums, parts):
    return [lax.ppermute(sums, "narrow", [(i, (i + off) % parts) for i in range(parts)]) for off in range(1, parts)]


def reduce_grads(b1, b2, groups, parts):
    ny = parts // 2
    rows1, rows2 = b1.shape[1], b2.shape[1]
    rows = rows1 + rows2
    chunk = rows // groups
    vmem = pl.BlockSpec(memory_space=pltpu.VMEM)
    dma = pltpu.SemaphoreType.DMA
    total = pl.pallas_call(
        reduce_kernel,
        in_specs=[vmem] * 2,
        out_specs=vmem,
        out_shape=jax.ShapeDtypeStruct((groups, chunk, 128), F32),
        scratch_shapes=[
            pltpu.VMEM((ny, rows, 128), F32),
            pltpu.VMEM((ny, rows, 128), F32),
            pltpu.VMEM((max(ny - 1, 1), rows, 128), F32),
            pltpu.VMEM((groups, chunk, 128), F32),
            pltpu.VMEM((groups, chunk, 128), F32),
            dma((2,)),
            dma((2,)),
            dma((ny,)),
            dma((ny,)),
            dma((2, groups)),
            dma((2, groups)),
        ],
        compiler_params=pltpu.CompilerParams(collective_id=0, has_side_effects=True, vmem_limit_bytes=40 * 2**20),
        name="reduce_gradients",
    )(b1.reshape(ny, 2, rows1, 128), b2.reshape(ny, 2, rows2, 128))
    return total.reshape(rows, 128)


def solution(mesh):
    series = P(("group", "narrow"), None)
    return jax.shard_map(
        functools.partial(on_device, mesh.shape["group"], mesh.shape["narrow"]),
        mesh=mesh,
        in_specs=(series, series, P(), P(), P(("group", "narrow"))) + (P(),) * 10 + (P(("group", "narrow"), None, None),),
        out_specs=(
            P(("group", "narrow"), None, None),
            P(("group", "narrow"), None, None),
            P(None, "narrow"),
            P("narrow"),
            P("narrow", None),
            P("narrow", None),
            P("narrow", None),
            P("narrow", None),
            P("narrow"),
            P(None, "narrow"),
            P(None, "narrow"),
            P("narrow", None),
        ),
        check_vma=False,
    )
```

profile of v0, /device:TPU:0, one launch (start us, length us, event | category | flops | bytes accessed | tf_op | source)
XLA Modules:
  0.0 218.3 jit_solution(10769611809835682144)
XLA Ops:
  0.6 0.7 fusion
  1.4 0.9 multiply_reduce_fusion
  2.3 0.1 multiply_reduce_fusion.1
  2.4 2.4 %collective-permute-start.2 = (f32[2,4]{1,0:T(2,128)S(1)}, f32[2,4]{1,0:T(2,128)S(1)}, u32[]{:S(2)}, u32[]{:S(2)}) collective-permute-start(f32[2,4]{1,0:T(2,128)S(1)} %multiply_reduce_fusion.1), channel_id=1, source_target_pairs={{0,3},{1,0},{2,1},{3,2},{4,7},{5,4},{6,5},{7,6},{8,11},{9,8},{10,9... | collective-permute-start | bytes 104 | tf_op jit(solution)/shard_map/ppermute | solution.py:619
  4.8 0.6 collective-permute-start.1
  5.4 0.2 collective-permute-start
  5.6 7.0 %split_weights_and_shift_lags.1 = (f32[4,96,1024]{2,1,0:T(8,128)}, bf16[144,288]{1,0:T(8,128)(2,1)}, bf16[432,432]{1,0:T(8,128)(2,1)}, bf16[144,432]{1,0:T(8,128...) custom-call(s32[84]{0:T(128)} %lag_ref.1, ...), custom_call_target="tpu_custom_call" | custom-call | flops 20000000 | bytes 8000000 | tf_op jit(solution)/shard_map/split_weights_and_shift_lags/pallas_call | solution.py:522
  12.6 0.0 collective-permute-done.2
  12.6 0.0 collective-permute-done.1
  12.7 0.0 collective-permute-done
  12.7 1.3 select_reduce_fusion.scale_ref
  14.0 82.9 %forward_and_ffn.1 = (f32[4,144,1024]{2,1,0:T(8,128)}, f32[4,144,1024]{2,1,0:T(8,128)}, f32[4,144,1024]{2,1,0:T(8,128)}, f32[4,144,1024]{2,1,0:T(8,128)}, f32[4,...) custom-call(f32[4]{0:T(128)} %select_reduce_fusion.scale_ref, ...), custom_call_target="tpu_custom_call" | custom-call | tf_op jit(solution)/shard_map/forward_and_ffn/pallas_call | solution.py:554
  96.9 0.0 copy-start.1
  96.9 87.3 %attention_backward.1 = (f32[4,144,1024]{2,1,0:T(8,128)}, f32[4,208,128]{2,1,0:T(8,128)}) custom-call(f32[4]{0:T(128)} %select_reduce_fusion.scale_ref, f32[4,144,1024]{2,1,0:T(8,128)} %get-tuple-element.55.q_ref, f32[4,144,1024]{2,1,0:T(8,128)} %get-tuple-element.56.k_ref, f32[4,144,1024]{2,1,0:T(8,128)} %get-tuple-element.57.v_ref, ...), custom_call_target="tpu_custom_call" | custom-call | tf_op jit(solution)/shard_map/attention_backward/pallas_call | solution.py:573
  184.3 0.0 copy-done.1
  184.3 0.0 copy-start.2
  184.3 1.0 copy-done.2
  185.3 30.1 %reduce_gradients.1 = f32[8,80,128]{2,1,0:T(8,128)S(1)} custom-call(f32[2,2,432,128]{3,2,1,0:T(8,128)S(1)} %bitcast.15, f32[2,2,208,128]{3,2,1,0:T(8,128)S(1)} %bitcast.16), custom_call_target="tpu_custom_call" | custom-call | tf_op jit(solution)/shard_map/reduce_gradients/pallas_call | solution.py:629
  215.4 0.0 copy-start
  215.4 0.7 copy-done
  216.1 2.0 unpack_gradients.1
  (3 shorter events, 0.0 us)
Async XLA Ops:
  2.4 10.3 %collective-permute-start.2 = (f32[2,4]{1,0:T(2,128)S(1)}, f32[2,4]{1,0:T(2,128)S(1)}, u32[]{:S(2)}, u32[]{:S(2)}) collective-permute-start(f32[2,4]{1,0:T(2,128)S(1)} %multiply_reduce_fusion.1), channel_id=1, source_target_pairs={{0,3},{1,0},{2,1},{3,2},{4,7},{5,4},{6,5},{7,6},{8,11},{9,8},{10,9... | collective-permute-start | bytes 104 | tf_op jit(solution)/shard_map/ppermute | solution.py:619
  4.8 7.9 %collective-permute-start.1 = (f32[2,4]{1,0:T(2,128)S(1)}, f32[2,4]{1,0:T(2,128)S(1)}, u32[]{:S(2)}, u32[]{:S(2)}) collective-permute-start(f32[2,4]{1,0:T(2,128)S(1)} %multiply_reduce_fusion.1), channel_id=1, source_target_pairs={{0,2},{1,3},{2,0},{3,1},{4,6},{5,7},{6,4},{7,5},{8,10},{9,11},{10,... | collective-permute-start | bytes 104 | tf_op jit(solution)/shard_map/ppermute | solution.py:619
  5.4 7.2 %collective-permute-start = (f32[2,4]{1,0:T(2,128)S(1)}, f32[2,4]{1,0:T(2,128)S(1)}, u32[]{:S(2)}, u32[]{:S(2)}) collective-permute-start(f32[2,4]{1,0:T(2,128)S(1)} %multiply_reduce_fusion.1), channel_id=1, source_target_pairs={{0,1},{1,2},{2,3},{3,0},{4,5},{5,6},{6,7},{7,4},{8,9},{9,10},{10,1... | collective-permute-start | bytes 104 | tf_op jit(solution)/shard_map/ppermute | solution.py:619
  96.9 87.4 %copy-start.1 = (f32[4,432,128]{2,1,0:T(8,128)S(1)}, f32[4,432,128]{2,1,0:T(8,128)}, u32[]{:S(2)}) copy-start(f32[4,432,128]{2,1,0:T(8,128)} %get-tuple-element.64) | copy-start | bytes 2654212
  184.3 1.0 copy-start.2
  215.4 0.7 copy-start
where the time goes:
time: 219 us; the launch traced here: 218 us
  Pallas kernels  209 us (95%)
  starting transfers between devices  3.24 us (1%)
  other arithmetic  3.08 us (1%)
    pallas_call x1, Pallas kernels, on_device(): pl.pallas_call(backward_kernel, grid=(n_series,), in_specs=[smem] + [each...  87.3 us
    pallas_call x1, Pallas kernels, on_device(): pl.pallas_call(forward_kernel, grid=(n_series,), in_specs=[smem, each(FPA...  82.9 us
    pallas_call x1, Pallas kernels, reduce_grads(): pl.pallas_call(reduce_kernel, in_specs=[vmem] * 2, out_specs=vmem, out_sh...  30.1 us
    pallas_call x1, Pallas kernels, on_device(): pl.pallas_call(prepare_kernel, in_specs=[smem] * 2 + [vmem] * 12, out_spe...  7.03 us
  transfers between devices with their start and end apart: 3, of which 0 were waited for; matrix products, arithmetic and copies ran while one was open for 0% of the time, Pallas kernels for 3%

commit v1 on v0

--- a/solution.py
+++ b/solution.py
@@ -13,10 +13,11 @@
 DSETS = 4
 FPAD = 96
 QB = 256
-TA = 512
-TC = 256
-TD = 256
+TA = 1024
+TC = 1024
+TD = 1024
 NLAG = 84
+AHEAD = 2
 
 NORM_EPS = 1e-05
 SCALE_EPS = 1e-05
@@ -125,7 +126,7 @@
             feat_ref[s, pl.ds(j, 1), :] = moved[s : s + 1]
         return missing + flag_ref[j].astype(F32) * (1.0 - moved[n_series:])
 
-    missing = lax.fori_loop(0, nlag, one_lag, jnp.zeros((n_series, t), F32), unroll=4)
+    missing = lax.fori_loop(0, nlag, one_lag, jnp.zeros((n_series, t), F32), unroll=12)
     for s in range(n_series):
         feat_ref[s, nlag : nlag + 1, :] = jnp.ones((1, t), F32)
         feat_ref[s, nlag + 1 : nlag + 2, :] = missing[s : s + 1] * nlag**-0.5
@@ -183,31 +184,52 @@
 
     causal = lax.broadcasted_iota(jnp.int32, (QB, QB), 0) <= lax.broadcasted_iota(jnp.int32, (QB, QB), 1)
 
-    def head(h, _):
-        rows = pl.ds(pl.multiple_of(h * HD, HD), HD)
+    def prepare(h):
+        rows = slice(h * HD, (h + 1) * HD)
         qh, ql = split(q_ref[0, rows, :])
         qc = jnp.concatenate([qh, ql, qh], axis=0)
         kh, kl = split(k_ref[0, rows, :])
         kh, kl = kh.astype(F32), kl.astype(F32)
         kc = jnp.concatenate([kh, kh, kl], axis=0).T.astype(BF16)
         vh, vl = split(v_ref[0, rows, :])
-        vs = jnp.concatenate([vh, vl], axis=0)
-        for block in range(t // QB):
-            lo, top = block * QB, (block + 1) * QB
-            s = nn(kc[:top], qc[:, lo:top])
-            last = jnp.where(causal, s[lo:], -1e30)
-            s = jnp.concatenate([s[:lo], last], axis=0) if block else last
-            m = jnp.max(s, axis=0, keepdims=True)
-            p = jnp.exp2(s - m)
-            total = jnp.sum(p, axis=0, keepdims=True)
+        return qc, kc, jnp.concatenate([vh, vl], axis=0), vh
+
+    def scores(sides, item):
+        qc, kc = sides[:2]
+        lo, top = item[1] * QB, (item[1] + 1) * QB
+        return nn(kc[:top], qc[:, lo:top])
+
+    def softmax(s, block):
+        lo = block * QB
+        last = jnp.where(causal, s[lo:], -1e30)
+        s = jnp.concatenate([s[:lo], last], axis=0) if block else last
+        return s, jnp.max(s, axis=0, keepdims=True)
+
+    def mix(sides, soft, item):
+        h, block = item
+        vs, vh = sides[2:]
+        s, m = soft
+        lo, top = block * QB, (block + 1) * QB
+        both = low = total = 0.0
+        for c in range(block + 1):
+            keys = slice(c * QB, (c + 1) * QB)
+            p = jnp.exp2(s[keys] - m)
+            total = total + jnp.sum(p, axis=0, keepdims=True)
             ph, pl_ = split(p)
-            both = nn(vs[:, :top], ph)
-            out = both[:HD] + both[HD:] + nn(vh[:, :top], pl_)
-            mixed_ref[rows, lo:top] = out / total
-            st_ref[0, pl.ds(h, 1), lo:top] = m + jnp.log2(total)
-        return 0
-
-    lax.fori_loop(0, HEADS, head, 0, unroll=3)
+            both = both + nn(vs[:, keys], ph)
+            low = low + nn(vh[:, keys], pl_)
+        mixed_ref[h * HD : (h + 1) * HD, lo:top] = (both[:HD] + both[HD:] + low) / total
+        st_ref[0, h : h + 1, lo:top] = m + jnp.log2(total)
+
+    sides = [prepare(h) for h in range(HEADS)]
+    items = [(h, block) for block in reversed(range(t // QB)) for h in range(HEADS)]
+    ahead = {}
+    for j in range(len(items) + AHEAD):
+        if j < len(items):
+            ahead[j] = scores(sides[items[j][0]], items[j])
+        if j >= AHEAD:
+            item = items[j - AHEAD]
+            mix(sides[item[0]], softmax(ahead.pop(j - AHEAD), item[1]), item)
 
     def feed(i, _):
         cols = pl.ds(pl.multiple_of(i * TC, TC), TC)
@@ -304,53 +326,65 @@
         tall = jnp.concatenate([hf, lf, hf, extras(-row)], axis=0).T.astype(BF16)
         return tall, jnp.concatenate([hi, lo], axis=0), hi
 
-    def head(h, _):
-        def rows_at(first):
-            return pl.ds(pl.multiple_of(first + h * HD, HD), HD)
-
-        rows = rows_at(0)
-        qc, qs, qh = sides(q_ref[0, rows, :], st_ref[0, pl.ds(h, 1), :])
-        mc, ms, mh = sides(dm_ref[0, rows, :], st_ref[0, pl.ds(16 + h, 1), :])
+    def rows_at(first, h):
+        return slice(first + h * HD, first + (h + 1) * HD)
+
+    def prepare(h):
+        rows = rows_at(0, h)
+        qc, qs, qh = sides(q_ref[0, rows, :], st_ref[0, h : h + 1, :])
+        mc, ms, mh = sides(dm_ref[0, rows, :], st_ref[0, 16 + h : 17 + h, :])
         kh, kl = split(k_ref[0, rows, :])
         kc = jnp.concatenate([kh, kh, kl, ones], axis=0)
-        ks = jnp.concatenate([kh, kl], axis=0)
         vh, vl = split(v_ref[0, rows, :])
         vc = jnp.concatenate([vh, vh, vl, ones], axis=0)
-
-        def scores(block):
-            lo = block * QB
-            cols = slice(lo, lo + QB)
-            return nn(qc[lo:], kc[:, cols]), nn(mc[lo:], vc[:, cols])
-
-        dq_blocks = [None] * nb
-        ahead = scores(0)
-        for block in range(nb):
-            lo = block * QB
-            cols = slice(lo, lo + QB)
-            s, dp = ahead
-            if block + 1 < nb:
-                ahead = scores(block + 1)
-            p = jnp.exp2(s)
-            first = jnp.where(causal, p[:QB], 0.0)
-            p = jnp.concatenate([first, p[QB:]], axis=0) if block + 1 < nb else first
-            ds = p * dp
-            ph, pl_ = split(p)
-            dh, dl = split(ds)
-            both = nn(ms[:, lo:], ph)
-            dqkv_ref[rows_at(2 * d), cols] = both[:HD] + both[HD:] + nn(mh[:, lo:], pl_)
-            both = nn(qs[:, lo:], dh)
-            dqkv_ref[rows_at(d), cols] = both[:HD] + both[HD:] + nn(qh[:, lo:], dl)
-            th, tl = split(ds.T)
-            both = nn(ks[:, cols], th)
-            part = both[:HD] + both[HD:] + nn(kh[:, cols], tl)
-            for i in range(block, nb):
-                piece = part[:, (i - block) * QB : (i - block + 1) * QB]
-                dq_blocks[i] = piece if dq_blocks[i] is None else dq_blocks[i] + piece
-        for i in range(nb):
-            dqkv_ref[rows, i * QB : (i + 1) * QB] = dq_blocks[i]
-        return 0
-
-    lax.fori_loop(0, HEADS, head, 0, unroll=3)
+        return qc, mc, kc, vc, qs, qh, ms, mh, jnp.concatenate([kh, kl], axis=0), kh
+
+    def tile(item):
+        h, kb, qb = item
+        return h, slice(kb * QB, (kb + 1) * QB), slice(qb * QB, (qb + 1) * QB)
+
+    def scores(item):
+        h, keys, steps = tile(item)
+        qc, mc, kc, vc = prepared[h][:4]
+        return nn(qc[steps], kc[:, keys]), nn(mc[steps], vc[:, keys])
+
+    def differentiate(item, s, dp):
+        h, keys, steps = tile(item)
+        kb, qb = item[1:]
+        qs, qh, ms, mh, ks, kh = prepared[h][4:]
+        p = jnp.exp2(s)
+        if kb == qb:
+            p = jnp.where(causal, p, 0.0)
+        ds = p * dp
+        ph, pl_ = split(p)
+        dh, dl = split(ds)
+        th, tl = split(ds.T)
+        both = nn(ms[:, steps], ph)
+        dv = both[:HD] + both[HD:] + nn(mh[:, steps], pl_)
+        both = nn(qs[:, steps], dh)
+        dk = both[:HD] + both[HD:] + nn(qh[:, steps], dl)
+        if qb > kb:
+            dk, dv = dk + sums[h][0], dv + sums[h][1]
+        sums[h] = dk, dv
+        if qb == nb - 1:
+            dqkv_ref[rows_at(d, h), keys] = dk
+            dqkv_ref[rows_at(2 * d, h), keys] = dv
+        both = nn(ks[:, keys], th)
+        dq = both[:HD] + both[HD:] + nn(kh[:, keys], tl)
+        if kb == qb:
+            dqkv_ref[rows_at(0, h), steps] = dq
+        else:
+            dqkv_ref[rows_at(0, h), steps] += dq
+
+    prepared = [prepare(h) for h in range(HEADS)]
+    sums = {}
+    items = [(h, kb, qb) for kb in reversed(range(nb)) for h in range(HEADS) for qb in range(kb, nb)]
+    ahead = {}
+    for j in range(len(items) + AHEAD):
+        if j < len(items):
+            ahead[j] = scores(items[j])
+        if j >= AHEAD:
+            differentiate(items[j - AHEAD], *ahead.pop(j - AHEAD))
 
     gain = gains[:, :1]
     scales = row_scales(scale_ref[step], NLAG)

time: 219 us -> 178 us (0.81)
  Pallas kernels: 209 us -> 168 us
    pallas_call x1, Pallas kernels: 82.9 us -> 60 us  [on_device(): pl.pallas_call(forward_kernel, grid=(n_series,), in_specs=[smem, each(FPA...]
    pallas_call x1, Pallas kernels: 87.3 us -> 70.2 us  [on_device(): pl.pallas_call(backward_kernel, grid=(n_series,), in_specs=[smem] + [each...]
where the time goes in v1:
time: 178 us; the launch traced here: 177 us
  Pallas kernels  168 us (94%)
  starting transfers between devices  3.24 us (2%)
  other arithmetic  3.08 us (2%)
    pallas_call x1, Pallas kernels, on_device(): pl.pallas_call(backward_kernel, grid=(n_series,), in_specs=[smem] + [each...  70.2 us
    pallas_call x1, Pallas kernels, on_device(): pl.pallas_call(forward_kernel, grid=(n_series,), in_specs=[smem, each(FPA...  60 us
    pallas_call x1, Pallas kernels, reduce_grads(): pl.pallas_call(reduce_kernel, in_specs=[vmem] * 2, out_specs=vmem, out_sh...  30.1 us
    pallas_call x1, Pallas kernels, on_device(): pl.pallas_call(prepare_kernel, in_specs=[smem] * 2 + [vmem] * 12, out_spe...  5.95 us
  transfers between devices with their start and end apart: 3, of which 0 were waited for; matrix products, arithmetic and copies ran while one was open for 0% of the time, Pallas kernels for 3%

profile of v1, /device:TPU:0, one launch (start us, length us, event | category | flops | bytes accessed | tf_op | source)
XLA Modules:
  0.0 177.2 jit_solution(8227717847296318050)
XLA Ops:
  0.6 0.7 fusion
  1.4 0.9 multiply_reduce_fusion
  2.3 0.1 multiply_reduce_fusion.1
  2.4 2.4 %collective-permute-start.2 = (f32[2,4]{1,0:T(2,128)S(1)}, f32[2,4]{1,0:T(2,128)S(1)}, u32[]{:S(2)}, u32[]{:S(2)}) collective-permute-start(f32[2,4]{1,0:T(2,128)S(1)} %multiply_reduce_fusion.1), channel_id=1, source_target_pairs={{0,3},{1,0},{2,1},{3,2},{4,7},{5,4},{6,5},{7,6},{8,11},{9,8},{10,9... | collective-permute-start | bytes 104 | tf_op jit(solution)/shard_map/ppermute | solution.py:653
  4.8 0.6 collective-permute-start.1
  5.4 0.2 collective-permute-start
  5.6 5.9 %split_weights_and_shift_lags.1 = (f32[4,96,1024]{2,1,0:T(8,128)}, bf16[144,288]{1,0:T(8,128)(2,1)}, bf16[432,432]{1,0:T(8,128)(2,1)}, bf16[144,432]{1,0:T(8,128...) custom-call(s32[84]{0:T(128)} %lag_ref.1, ...), custom_call_target="tpu_custom_call" | custom-call | flops 20000000 | bytes 8000000 | tf_op jit(solution)/shard_map/split_weights_and_shift_lags/pallas_call | solution.py:556
  11.6 0.0 collective-permute-done.2
  11.6 0.0 collective-permute-done.1
  11.6 0.0 collective-permute-done
  11.6 1.3 select_reduce_fusion.scale_ref
  13.0 60.0 %forward_and_ffn.1 = (f32[4,144,1024]{2,1,0:T(8,128)}, f32[4,144,1024]{2,1,0:T(8,128)}, f32[4,144,1024]{2,1,0:T(8,128)}, f32[4,144,1024]{2,1,0:T(8,128)}, f32[4,...) custom-call(f32[4]{0:T(128)} %select_reduce_fusion.scale_ref, ...), custom_call_target="tpu_custom_call" | custom-call | tf_op jit(solution)/shard_map/forward_and_ffn/pallas_call | solution.py:588
  72.9 0.0 copy-start.1
  72.9 70.2 %attention_backward.1 = (f32[4,144,1024]{2,1,0:T(8,128)}, f32[4,208,128]{2,1,0:T(8,128)}) custom-call(f32[4]{0:T(128)} %select_reduce_fusion.scale_ref, f32[4,144,1024]{2,1,0:T(8,128)} %get-tuple-element.55.q_ref, f32[4,144,1024]{2,1,0:T(8,128)} %get-tuple-element.56.k_ref, f32[4,144,1024]{2,1,0:T(8,128)} %get-tuple-element.57.v_ref, ...), custom_call_target="tpu_custom_call" | custom-call | tf_op jit(solution)/shard_map/attention_backward/pallas_call | solution.py:607
  143.1 0.0 copy-done.1
  143.1 0.0 copy-start.2
  143.2 1.0 copy-done.2
  144.2 30.1 %reduce_gradients.1 = f32[8,80,128]{2,1,0:T(8,128)S(1)} custom-call(f32[2,2,432,128]{3,2,1,0:T(8,128)S(1)} %bitcast.15, f32[2,2,208,128]{3,2,1,0:T(8,128)S(1)} %bitcast.16), custom_call_target="tpu_custom_call" | custom-call | tf_op jit(solution)/shard_map/reduce_gradients/pallas_call | solution.py:663
  174.3 0.0 copy-start
  174.3 0.7 copy-done
  175.0 2.0 %unpack_gradients.1 = (f32[36,86]{1,0:T(8,128)}, f32[36]{0:T(128)}, f32[36,144]{1,0:T(8,128)}, f32[36,144]{1,0:T(8,128)}, f32[36,144]{1,0:T(8,128)}, /*index=5*/...) custom-call(f32[640,128]{1,0:T(8,128)} %bitcast.14), custom_call_target="tpu_custom_call" | custom-call | tf_op jit(solution)/shard_map/unpack_gradients/pallas_call | solution.py:624
  (3 shorter events, 0.0 us)
Async XLA Ops:
  2.4 9.2 %collective-permute-start.2 = (f32[2,4]{1,0:T(2,128)S(1)}, f32[2,4]{1,0:T(2,128)S(1)}, u32[]{:S(2)}, u32[]{:S(2)}) collective-permute-start(f32[2,4]{1,0:T(2,128)S(1)} %multiply_reduce_fusion.1), channel_id=1, source_target_pairs={{0,3},{1,0},{2,1},{3,2},{4,7},{5,4},{6,5},{7,6},{8,11},{9,8},{10,9... | collective-permute-start | bytes 104 | tf_op jit(solution)/shard_map/ppermute | solution.py:653
  4.8 6.8 %collective-permute-start.1 = (f32[2,4]{1,0:T(2,128)S(1)}, f32[2,4]{1,0:T(2,128)S(1)}, u32[]{:S(2)}, u32[]{:S(2)}) collective-permute-start(f32[2,4]{1,0:T(2,128)S(1)} %multiply_reduce_fusion.1), channel_id=1, source_target_pairs={{0,2},{1,3},{2,0},{3,1},{4,6},{5,7},{6,4},{7,5},{8,10},{9,11},{10,... | collective-permute-start | bytes 104 | tf_op jit(solution)/shard_map/ppermute | solution.py:653
  5.4 6.1 %collective-permute-start = (f32[2,4]{1,0:T(2,128)S(1)}, f32[2,4]{1,0:T(2,128)S(1)}, u32[]{:S(2)}, u32[]{:S(2)}) collective-permute-start(f32[2,4]{1,0:T(2,128)S(1)} %multiply_reduce_fusion.1), channel_id=1, source_target_pairs={{0,1},{1,2},{2,3},{3,0},{4,5},{5,6},{6,7},{7,4},{8,9},{9,10},{10,1... | collective-permute-start | bytes 104 | tf_op jit(solution)/shard_map/ppermute | solution.py:653
  72.9 70.2 %copy-start.1 = (f32[4,432,128]{2,1,0:T(8,128)S(1)}, f32[4,432,128]{2,1,0:T(8,128)}, u32[]{:S(2)}) copy-start(f32[4,432,128]{2,1,0:T(8,128)} %get-tuple-element.64) | copy-start | bytes 2654212
  143.1 1.0 copy-start.2
  174.3 0.7 copy-start

commit v2 on v1

--- a/solution.py
+++ b/solution.py
@@ -270,40 +270,136 @@
 
     @pl.when(step == pl.num_programs(0) - 1)
     def _():
-        parts = b1_ref.shape[0]
+        parts = 2 * b1_ref.shape[0]
         fs, ds = ff // parts, d // parts
         g_gu_t = g_gu[...].T
         g_down_t = g_down[...].T
         g_out_t = g_out[...].T
         gf = jnp.sum(g_gf[...], axis=1, keepdims=True)
-        b1_ref[...] = jnp.zeros_like(b1_ref)
         for n in range(parts):
             gf_own = jnp.concatenate([gf[n * ds : (n + 1) * ds], jnp.zeros((d - ds, 1), F32)], axis=0)
             share = jnp.concatenate([
                 g_gu_t[:, n * fs : (n + 1) * fs], g_gu_t[:, ff + n * fs : ff + (n + 1) * fs],
                 g_down_t[:, n * fs : (n + 1) * fs], g_out_t[:, n * ds : (n + 1) * ds], gf_own,
             ], axis=1)
-            put_share(b1_ref, n, share)
-
-
-def put_share(ref, n, share):
+            b1_ref[n // 2, n % 2] = stack_columns(share, b1_ref.shape[2])
+
+
+def stack_columns(share, height):
     rows, cols = share.shape
-    pad_rows, pad_cols = -rows % 8, -cols % 128
-    if pad_rows:
-        share = jnp.concatenate([share, jnp.zeros((pad_rows, cols), F32)], axis=0)
+    pad_cols = -cols % 128
     if pad_cols:
-        share = jnp.concatenate([share, jnp.zeros((share.shape[0], pad_cols), F32)], axis=1)
-    height = share.shape[0]
-    for c in range(share.shape[1] // 128):
-        ref[n, c * height : (c + 1) * height, :] = share[:, c * 128 : (c + 1) * 128]
+        share = jnp.concatenate([share, jnp.zeros((rows, pad_cols), F32)], axis=1)
+    pieces = [share[:, c * 128 : (c + 1) * 128] for c in range(share.shape[1] // 128)]
+    left = height - len(pieces) * rows
+    if left:
+        pieces.append(jnp.zeros((left, 128), F32))
+    return jnp.concatenate(pieces, axis=0)
+
+
+def at(group, narrow):
+    return (group, narrow)
+
+
+def greet(groups, ny):
+    g, n = lax.axis_index("group"), lax.axis_index("narrow")
+    core, y = lax.rem(n, 2), lax.div(n, 2)
+    barrier = pltpu.get_barrier_semaphore()
+    peers = [at(g, y * 2 + 1 - core)]
+    peers += [at(g, lax.rem(y + off, ny) * 2 + core) for off in range(1, ny)]
+    peers += [at(lax.rem(g + off, groups), n) for off in range(1, groups)]
+    for peer in peers:
+        pl.semaphore_signal(barrier, inc=1, device_id=peer, device_id_type=pl.DeviceIdType.MESH)
+    pl.semaphore_wait(barrier, len(peers))
+
+
+def share_phases(src, total_ref, base, recv1, pair, recv2, share, recv3, send_sem, recv_sem):
+    ny, rows = src.shape[0], src.shape[2]
+    groups, chunk = recv3.shape[0], recv3.shape[1]
+    g, n = lax.axis_index("group"), lax.axis_index("narrow")
+    core, y = lax.rem(n, 2), lax.div(n, 2)
+
+    def copy(i, source, target, to):
+        return pltpu.make_async_remote_copy(
+            src_ref=source, dst_ref=target, send_sem=send_sem.at[i], recv_sem=recv_sem.at[i], device_id=to,
+            device_id_type=pl.DeviceIdType.MESH,
+        )
+
+    def over_core():
+        return [copy(0, src.at[:, 1 - core], recv1, at(g, y * 2 + 1 - core))]
+
+    def over_y():
+        peers = [lax.rem(y + off, ny) for off in range(1, ny)]
+        return [copy(1 + i, pair.at[p], recv2.at[i], at(g, p * 2 + core)) for i, p in enumerate(peers)]
+
+    def over_group():
+        peers = [lax.rem(g + off, groups) for off in range(1, groups)]
+        return [copy(ny + i, share.at[p], recv3.at[1 + i], at(p, n)) for i, p in enumerate(peers)]
+
+    def gather():
+        own = total_ref.at[g, pl.ds(base, chunk)]
+        peers = [lax.rem(g + off, groups) for off in range(1, groups)]
+        return [copy(ny + groups - 1 + i, own, own, at(p, n)) for i, p in enumerate(peers)]
+
+    def start(copies):
+        for c in copies:
+            c.start()
+
+    def arrive(copies):
+        for c in copies:
+            c.wait_recv()
+
+    def one():
+        start(over_core())
+
+    def two():
+        arrive(over_core())
+        for i in range(ny):
+            pair[i] = src[i, core] + recv1[i]
+        start(over_y())
+
+    def three():
+        arrive(over_y())
+        total = pair[y]
+        for i in range(ny - 1):
+            total += recv2[i]
+        share[...] = total.reshape(groups, chunk, 128)
+        start(over_group())
+
+    def four():
+        recv3[0] = share[g]
+        arrive(over_group())
+        total_ref[g, base : base + chunk] = jnp.sum(recv3[...], axis=0)
+        start(gather())
+
+    def five():
+        arrive(gather())
+        for copies in (over_core(), over_y(), over_group(), gather()):
+            for c in copies:
+                c.wait_send()
+
+    return one, two, three, four, five
 
 
 def backward_kernel(
-    scale_ref, q_ref, k_ref, v_ref, dm_ref, st_ref, da_ref, x_ref, feat_ref, w_dqkv, gains, cos_ref, sin_ref,
-    dx_ref, b2_ref,
-    dqkv_ref, g_qkv, g_in, g_ga,
+    dx_steps, scale_ref, q_ref, k_ref, v_ref, dm_ref, st_ref, da_ref, x_ref, feat_ref, w_dqkv, gains, cos_ref, sin_ref, b1_ref,
+    dx_ref, out_ref,
+    dqkv_ref, g_qkv, g_in, g_ga, b2_ref, total_ref, *buffers,
 ):
     step = pl.program_id(0)
+    early = share_phases(b1_ref, total_ref, 0, *buffers[:7])
+    late = share_phases(b2_ref, total_ref, b1_ref.shape[2] // total_ref.shape[0], *buffers[7:])
+
+    @pl.when(step == 0)
+    def _():
+        greet(total_ref.shape[0], b1_ref.shape[0])
+
+    for i, phase in enumerate(early[:4]):
+
+        @pl.when(step == min(i, dx_steps - 1))
+        def _():
+            phase()
+
     d, t = q_ref.shape[1], q_ref.shape[2]
 
     @pl.when(step == 0)
@@ -412,102 +508,45 @@
 
     @pl.when(step == pl.num_programs(0) - 1)
     def _():
-        parts = b2_ref.shape[0]
+        parts = 2 * b2_ref.shape[0]
         ds = d // parts
         g_qkv_t = g_qkv[...].T
         ga = jnp.sum(g_ga[...], axis=1, keepdims=True)
-        b2_ref[...] = jnp.zeros_like(b2_ref)
         for n in range(parts):
             own = slice(n * ds, (n + 1) * ds)
-            put_share(b2_ref, n, jnp.concatenate([g_qkv_t[own], g_in[own, :], ga[own]], axis=1))
-
-
-def reduce_kernel(b1_ref, b2_ref, out_ref, recv1, pair, recv2, share, recv3, sem_s, sem_r, gsem_s, gsem_r, hsem_s, hsem_r):
-    ny = b1_ref.shape[0]
-    r1, r2 = b1_ref.shape[2], b2_ref.shape[2]
-    groups, chunk = recv3.shape[0], recv3.shape[1]
-    g = lax.axis_index("group")
-    n = lax.axis_index("narrow")
-    core, y = lax.rem(n, 2), lax.div(n, 2)
-    other = 1 - core
-
-    def at(group, narrow):
-        return (group, narrow)
-
-    mesh_id = pl.DeviceIdType.MESH
-    barrier = pltpu.get_barrier_semaphore()
-    pl.semaphore_signal(barrier, inc=1, device_id=at(g, y * 2 + other), device_id_type=mesh_id)
-    for off in range(1, ny):
-        peer = lax.rem(y + off, ny)
-        pl.semaphore_signal(barrier, inc=1, device_id=at(g, peer * 2 + core), device_id_type=mesh_id)
-    for off in range(1, groups):
-        pl.semaphore_signal(barrier, inc=1, device_id=at(lax.rem(g + off, groups), n), device_id_type=mesh_id)
-    pl.semaphore_wait(barrier, 1 + (ny - 1) + (groups - 1))
-
-    def copy(src, dst, send, recv, to):
-        return pltpu.make_async_remote_copy(
-            src_ref=src, dst_ref=dst, send_sem=send, recv_sem=recv, device_id=to, device_id_type=mesh_id
-        )
-
-    sibling = at(g, y * 2 + other)
-    first = copy(b1_ref.at[:, other], recv1.at[:, pl.ds(0, r1)], sem_s.at[0], sem_r.at[0], sibling)
-    second = copy(b2_ref.at[:, other], recv1.at[:, pl.ds(r1, r2)], sem_s.at[1], sem_r.at[1], sibling)
-    first.start()
-    second.start()
-    first.wait_recv()
-    second.wait_recv()
-    for i in range(ny):
-        pair[i, :r1] = b1_ref[i, core] + recv1[i, :r1]
-        pair[i, r1 : r1 + r2] = b2_ref[i, core] + recv1[i, r1 : r1 + r2]
-
-    sends = []
-    for off in range(1, ny):
-        peer = lax.rem(y + off, ny)
-        sends.append(copy(pair.at[peer], recv2.at[off - 1], gsem_s.at[off], gsem_r.at[off], at(g, peer * 2 + core)))
-        sends[-1].start()
-    for s in sends:
-        s.wait_recv()
-    total = pair[y]
-    for off in range(1, ny):
-        total += recv2[off - 1]
-    share[...] = total.reshape(share.shape)
-
-    sends_b = []
-    for off in range(1, groups):
-        peer = lax.rem(g + off, groups)
-        sends_b.append(copy(share.at[peer], recv3.at[off], hsem_s.at[0, off], hsem_r.at[0, off], at(peer, n)))
-        sends_b[-1].start()
-    recv3[0] = share[g]
-    for s in sends_b:
-        s.wait_recv()
-    out_ref[g] = jnp.sum(recv3[...], axis=0)
-    sends_c = []
-    for off in range(1, groups):
-        peer = lax.rem(g + off, groups)
-        sends_c.append(copy(out_ref.at[g], out_ref.at[g], hsem_s.at[1, off], hsem_r.at[1, off], at(peer, n)))
-        sends_c[-1].start()
-    for s in sends_c:
-        s.wait_recv()
-    for s in [first, second] + sends + sends_b + sends_c:
-        s.wait_send()
-
-
-def unpack_kernel(
-    total_ref, g_in, g_ga, g_q, g_k, g_v, g_out, g_gf, g_gate, g_up, g_down,
-):
+            share = jnp.concatenate([g_qkv_t[own], g_in[own, :], ga[own]], axis=1)
+            b2_ref[n // 2, n % 2] = stack_columns(share, b2_ref.shape[2])
+        for phase in late[:4]:
+            phase()
+        for end in (early[4], late[4]):
+            end()
+        out_ref[...] = total_ref[...]
+
+
+def unpack_kernel(total_ref, dx_ref, dx_out, *grads):
+    dx_out[...] = dx_ref[...]
+
+    @pl.when(pl.program_id(0) == 0)
+    def _():
+        unpack(total_ref, *grads)
+
+
+def unpack(total_ref, g_in, g_ga, g_q, g_k, g_v, g_out, g_gf, g_gate, g_up, g_down):
     d, fs = g_gate.shape
     ds, nf = g_in.shape
+    groups = total_ref.shape[0]
     wide = round_up(3 * fs + ds + 1, 128) // 128
-    one = jnp.concatenate([total_ref[c * d : (c + 1) * d, :] for c in range(wide)], axis=1)
+    c1 = round_up(wide * d, 8 * groups) // groups
+    one = jnp.concatenate([total_ref[g, :c1] for g in range(groups)], axis=0)
+    one = jnp.concatenate([one[c * d : (c + 1) * d, :] for c in range(wide)], axis=1)
     g_gate[...] = one[:, :fs]
     g_up[...] = one[:, fs : 2 * fs]
     g_down[...] = one[:, 2 * fs : 3 * fs]
     g_out[...] = one[:, 3 * fs : 3 * fs + ds].T
     g_gf[...] = one[:ds, 3 * fs + ds]
-    base = wide * d
-    height = round_up(ds, 8)
     wide = round_up(3 * d + FPAD + 1, 128) // 128
-    two = jnp.concatenate([total_ref[base + c * height : base + c * height + ds, :] for c in range(wide)], axis=1)
+    two = jnp.concatenate([total_ref[g, c1:] for g in range(groups)], axis=0)
+    two = jnp.concatenate([two[c * ds : (c + 1) * ds, :] for c in range(wide)], axis=1)
     g_q[...] = two[:, :d]
     g_k[...] = two[:, d : 2 * d]
     g_v[...] = two[:, 2 * d : 3 * d]
@@ -580,11 +619,10 @@
     set_scale = sums[0] / jnp.maximum(sums[1], 1.0) + SCALE_EPS
     series_scale = jnp.sum(onehot * set_scale[None, :], axis=1)
 
-    rows1 = round_up(3 * fs + ds + 1, 128) // 128 * d
-    rows2 = round_up(3 * d + FPAD + 1, 128) // 128 * round_up(ds, 8)
-    rows2 = round_up(rows1 + rows2, 8 * groups) - rows1
+    rows1 = round_up(round_up(3 * fs + ds + 1, 128) // 128 * d, 8 * groups)
+    rows2 = round_up(round_up(3 * d + FPAD + 1, 128) // 128 * ds, 8 * groups)
     full = [w_in, w_qkv, w_out, w_gu, w_down, w_dh, w_dgu, w_dm, gains, cos, sin]
-    b1 = shape(parts, rows1, 128)
+    b1 = shape(parts // 2, 2, rows1, 128)
     act, q, k, v, dm, st, da, x, b1 = pl.pallas_call(
         forward_kernel,
         grid=(n_series,),
@@ -602,36 +640,57 @@
         name="forward_and_ffn",
     )(series_scale, raw, *full, jnp.transpose(cotangent, (0, 2, 1)))
 
-    b2 = shape(parts, rows2, 128)
-    full = [w_dqkv, gains, cos, sin]
-    dx, b2 = pl.pallas_call(
-        backward_kernel,
+    ny = parts // 2
+    c1, c2 = rows1 // groups, rows2 // groups
+    total = shape(groups, c1 + c2, 128)
+    full = [w_dqkv, gains, cos, sin, b1]
+    copies = ny + 2 * (groups - 1)
+    dma = pltpu.SemaphoreType.DMA
+    buffers = []
+    for rows, chunk in ((rows1, c1), (rows2, c2)):
+        buffers += [
+            pltpu.VMEM((ny, rows, 128), F32),
+            pltpu.VMEM((ny, rows, 128), F32),
+            pltpu.VMEM((max(ny - 1, 1), rows, 128), F32),
+            pltpu.VMEM((groups, chunk, 128), F32),
+            pltpu.VMEM((groups, chunk, 128), F32),
+            dma((copies,)),
+            dma((copies,)),
+        ]
+    dx, total = pl.pallas_call(
+        functools.partial(backward_kernel, n_series),
         grid=(n_series,),
         in_specs=[smem] + [each(d)] * 4 + [each(32)] + [each(d)] * 2 + [each(FPAD)] + [whole(a) for a in full],
-        out_specs=[each(d), whole(b2)],
-        out_shape=[shape(n_series, d, t), b2],
+        out_specs=[each(d), whole(total)],
+        out_shape=[shape(n_series, d, t), total],
         scratch_shapes=[
             pltpu.VMEM((3 * d, t), F32),
             pltpu.VMEM((3 * d, d), F32),
             pltpu.VMEM((d, FPAD), F32),
             pltpu.VMEM((d, 128), F32),
+            pltpu.VMEM((ny, 2, rows2, 128), F32),
+            pltpu.VMEM((groups, c1 + c2, 128), F32),
+            *buffers,
         ],
+        compiler_params=pltpu.CompilerParams(
+            dimension_semantics=("arbitrary",), vmem_limit_bytes=62 * 2**20, collective_id=0, has_side_effects=True
+        ),
+        name="attention_backward_and_sums",
+    )(series_scale, q, k, v, dm, st, da, x, raw, *full)
+
+    grads = [
+        shape(ds, nf), shape(ds), shape(ds, d), shape(ds, d), shape(ds, d), shape(ds, d), shape(ds),
+        shape(d, fs), shape(d, fs), shape(d, fs),
+    ]
+    dx, *grads = pl.pallas_call(
+        unpack_kernel,
+        grid=(n_series,),
+        in_specs=[whole(total), each(d)],
+        out_specs=[each(d)] + [whole(a) for a in grads],
+        out_shape=[shape(n_series, d, t)] + grads,
         compiler_params=params,
-        name="attention_backward",
-    )(series_scale, q, k, v, dm, st, da, x, raw, *full)
-
-    total = reduce_grads(b1, b2, groups, parts)
-    grads = pl.pallas_call(
-        unpack_kernel,
-        in_specs=[vmem],
-        out_specs=[vmem] * 10,
-        out_shape=[
-            shape(ds, nf), shape(ds), shape(ds, d), shape(ds, d), shape(ds, d), shape(ds, d), shape(ds),
-            shape(d, fs), shape(d, fs), shape(d, fs),
-        ],
-        compiler_params=plain,
         name="unpack_gradients",
-    )(total)
+    )(total, dx)
     return (
         jnp.transpose(act, (0, 2, 1)),
         jnp.transpose(dx, (0, 2, 1)),
@@ -651,37 +710,6 @@
 
 def exchange_sums(sums, parts):
     return [lax.ppermute(sums, "narrow", [(i, (i + off) % parts) for i in range(parts)]) for off in range(1, parts)]
-
-
-def reduce_grads(b1, b2, groups, parts):
-    ny = parts // 2
-    rows1, rows2 = b1.shape[1], b2.shape[1]
-    rows = rows1 + rows2
-    chunk = rows // groups
-    vmem = pl.BlockSpec(memory_space=pltpu.VMEM)
-    dma = pltpu.SemaphoreType.DMA
-    total = pl.pallas_call(
-        reduce_kernel,
-        in_specs=[vmem] * 2,
-        out_specs=vmem,
-        out_shape=jax.ShapeDtypeStruct((groups, chunk, 128), F32),
-        scratch_shapes=[
-            pltpu.VMEM((ny, rows, 128), F32),
-            pltpu.VMEM((ny, rows, 128), F32),
-            pltpu.VMEM((max(ny - 1, 1), rows, 128), F32),
-            pltpu.VMEM((groups, chunk, 128), F32),
-            pltpu.VMEM((groups, chunk, 128), F32),
-            dma((2,)),
-            dma((2,)),
-            dma((ny,)),
-            dma((ny,)),
-            dma((2, groups)),
-            dma((2, groups)),
-        ],
-        compiler_params=pltpu.CompilerParams(collective_id=0, has_side_effects=True, vmem_limit_bytes=40 * 2**20),
-        name="reduce_gradients",
-    )(b1.reshape(ny, 2, rows1, 128), b2.reshape(ny, 2, rows2, 128))
-    return total.reshape(rows, 128)
 
 
 def solution(mesh):

time: 178 us -> 169 us (0.949)
  Pallas kernels: 168 us -> 161 us
    pallas_call x3 -> x2, Pallas kernels: 102 us -> 95.2 us  [the longest x1 90.6 us: on_device(): pl.pallas_call(functools.partial(backward_kernel, n_series), grid=(n_seri...]
  transfers between devices with their start and end apart: 3 -> 3, of which waited for: 0 -> 0; matrix products, arithmetic and copies ran while one was open for 0% -> 0% of each run, Pallas kernels for 3% -> 4%
where the time goes in v2:
time: 169 us; the launch traced here: 168 us
  Pallas kernels  161 us (95%)
  starting transfers between devices  3.24 us (2%)
  other arithmetic  3.08 us (2%)
    pallas_call x1, Pallas kernels, on_device(): pl.pallas_call(functools.partial(backward_kernel, n_series), grid=(n_seri...  90.6 us
    pallas_call x1, Pallas kernels, on_device(): pl.pallas_call(forward_kernel, grid=(n_series,), in_specs=[smem, each(FPA...  60 us
    pallas_call x1, Pallas kernels, on_device(): pl.pallas_call(prepare_kernel, in_specs=[smem] * 2 + [vmem] * 12, out_spe...  6.04 us
    pallas_call x1, Pallas kernels, on_device(): pl.pallas_call(unpack_kernel, grid=(n_series,), in_specs=[whole(total), e...  4.53 us
  transfers between devices with their start and end apart: 3, of which 0 were waited for; matrix products, arithmetic and copies ran while one was open for 0% of the time, Pallas kernels for 4%

profile of v2, /device:TPU:0, one launch (start us, length us, event | category | flops | bytes accessed | tf_op | source)
XLA Modules:
  0.0 168.3 jit_solution(5839720761252933250)
XLA Ops:
  0.6 0.7 fusion
  1.4 0.9 multiply_reduce_fusion
  2.3 0.1 multiply_reduce_fusion.1
  2.4 2.4 %collective-permute-start.2 = (f32[2,4]{1,0:T(2,128)S(1)}, f32[2,4]{1,0:T(2,128)S(1)}, u32[]{:S(2)}, u32[]{:S(2)}) collective-permute-start(f32[2,4]{1,0:T(2,128)S(1)} %multiply_reduce_fusion.1), channel_id=1, source_target_pairs={{0,3},{1,0},{2,1},{3,2},{4,7},{5,4},{6,5},{7,6},{8,11},{9,8},{10,9... | collective-permute-start | bytes 104 | tf_op jit(solution)/shard_map/ppermute | solution.py:712
  4.8 0.6 collective-permute-start.1
  5.4 0.2 collective-permute-start
  5.6 6.0 %split_weights_and_shift_lags.1 = (f32[4,96,1024]{2,1,0:T(8,128)}, bf16[144,288]{1,0:T(8,128)(2,1)}, bf16[432,432]{1,0:T(8,128)(2,1)}, bf16[144,432]{1,0:T(8,128...) custom-call(s32[84]{0:T(128)} %lag_ref.1, ...), custom_call_target="tpu_custom_call" | custom-call | flops 20000000 | bytes 8000000 | tf_op jit(solution)/shard_map/split_weights_and_shift_lags/pallas_call | solution.py:595
  11.7 0.0 collective-permute-done.2
  11.7 0.0 collective-permute-done.1
  11.7 0.0 collective-permute-done
  11.7 1.3 select_reduce_fusion.scale_ref
  13.1 60.0 %forward_and_ffn.1 = (f32[4,144,1024]{2,1,0:T(8,128)}, f32[4,144,1024]{2,1,0:T(8,128)}, f32[4,144,1024]{2,1,0:T(8,128)}, f32[4,144,1024]{2,1,0:T(8,128)}, f32[4,...) custom-call(f32[4]{0:T(128)} %select_reduce_fusion.scale_ref, ...), custom_call_target="tpu_custom_call" | custom-call | tf_op jit(solution)/shard_map/forward_and_ffn/pallas_call | solution.py:626
  73.0 90.6 %attention_backward_and_sums.1 = (f32[4,144,1024]{2,1,0:T(8,128)}, f32[8,80,128]{2,1,0:T(8,128)}) custom-call(f32[4]{0:T(128)} %select_reduce_fusion.scale_ref, f32[4,144,1024]{2,1,0:T(8,128)} %get-tuple-element.56.q_ref, f32[4,144,1024]{2,1,0:T(8,128)} %get-tuple-element.57.k_ref, f32[4,144,1024]{2,1,0:T(8,128)} %get-tuple-element.58.v_ref, ...), custom_call_target="tpu_custom_call" | custom-call | tf_op jit(solution)/shard_map/attention_backward_and_sums/pallas_call | solution.py:660
  163.7 4.5 %unpack_gradients.1 = (f32[4,144,1024]{2,1,0:T(8,128)}, f32[36,86]{1,0:T(8,128)}, f32[36]{0:T(128)}, f32[36,144]{1,0:T(8,128)}, f32[36,144]{1,0:T(8,128)}, /*ind...) custom-call(f32[8,80,128]{2,1,0:T(8,128)} %get-tuple-element.65.tota, ...), custom_call_target="tpu_custom_call" | custom-call | tf_op jit(solution)/shard_map/unpack_gradients/pallas_call | solution.py:685
  (3 shorter events, 0.0 us)
Async XLA Ops:
  2.4 9.3 %collective-permute-start.2 = (f32[2,4]{1,0:T(2,128)S(1)}, f32[2,4]{1,0:T(2,128)S(1)}, u32[]{:S(2)}, u32[]{:S(2)}) collective-permute-start(f32[2,4]{1,0:T(2,128)S(1)} %multiply_reduce_fusion.1), channel_id=1, source_target_pairs={{0,3},{1,0},{2,1},{3,2},{4,7},{5,4},{6,5},{7,6},{8,11},{9,8},{10,9... | collective-permute-start | bytes 104 | tf_op jit(solution)/shard_map/ppermute | solution.py:712
  4.8 6.9 %collective-permute-start.1 = (f32[2,4]{1,0:T(2,128)S(1)}, f32[2,4]{1,0:T(2,128)S(1)}, u32[]{:S(2)}, u32[]{:S(2)}) collective-permute-start(f32[2,4]{1,0:T(2,128)S(1)} %multiply_reduce_fusion.1), channel_id=1, source_target_pairs={{0,2},{1,3},{2,0},{3,1},{4,6},{5,7},{6,4},{7,5},{8,10},{9,11},{10,... | collective-permute-start | bytes 104 | tf_op jit(solution)/shard_map/ppermute | solution.py:712
  5.4 6.2 %collective-permute-start = (f32[2,4]{1,0:T(2,128)S(1)}, f32[2,4]{1,0:T(2,128)S(1)}, u32[]{:S(2)}, u32[]{:S(2)}) collective-permute-start(f32[2,4]{1,0:T(2,128)S(1)} %multiply_reduce_fusion.1), channel_id=1, source_target_pairs={{0,1},{1,2},{2,3},{3,0},{4,5},{5,6},{6,7},{7,4},{8,9},{9,10},{10,1... | collective-permute-start | bytes 104 | tf_op jit(solution)/shard_map/ppermute | solution.py:712

commit v3 on v2

--- a/solution.py
+++ b/solution.py
@@ -102,14 +102,16 @@
 
 def row_scales(scale, nlag):
     row = lax.broadcasted_iota(jnp.int32, (FPAD, 128), 0)
-    scales = jnp.full((FPAD, 128), scale, F32)
+    scales = jnp.broadcast_to(scale, (FPAD, 128))
     inverse, logs = 1.0 / scales, jnp.log(scales)
     return jnp.where(row < nlag, inverse, jnp.where(row == nlag, logs, 1.0))[:, :1]
 
 
 def prepare_kernel(
-    lag_ref, flag_ref, vals_ref, obs_ref, in_ref, wq_ref, wk_ref, wv_ref, wo_ref, wg_ref, wu_ref, wd_ref, ga_ref, gf_ref,
-    feat_ref, w_in, w_qkv, w_out, w_gu, w_down, w_dh, w_dgu, w_dm, w_dqkv, gains,
+    parts, lag_ref, flag_ref, ids_ref, vals_ref, obs_ref, in_ref, wq_ref, wk_ref, wv_ref, wo_ref, wg_ref, wu_ref, wd_ref,
+    ga_ref, gf_ref,
+    scale_ref, feat_ref, w_in, w_qkv, w_out, w_gu, w_down, w_dh, w_dgu, w_dm, w_dqkv, gains,
+    own, others, send_sem, recv_sem,
 ):
     n_series, t = vals_ref.shape
     d, nf = in_ref.shape
@@ -117,6 +119,29 @@
     ff = wg_ref.shape[1]
     obs = obs_ref[...].astype(F32)
     both = jnp.concatenate([vals_ref[...] * obs, obs], axis=0)
+
+    g, n = lax.axis_index("group"), lax.axis_index("narrow")
+    barrier = pltpu.get_barrier_semaphore()
+    copies = []
+    for off in range(1, parts):
+        peer = (g, lax.rem(n + off, parts))
+        pl.semaphore_signal(barrier, inc=1, device_id=peer, device_id_type=pl.DeviceIdType.MESH)
+        copies.append(pltpu.make_async_remote_copy(
+            src_ref=own, dst_ref=others.at[off - 1], send_sem=send_sem.at[off - 1], recv_sem=recv_sem.at[off - 1],
+            device_id=peer, device_id_type=pl.DeviceIdType.MESH,
+        ))
+    series = lax.broadcasted_iota(jnp.int32, (n_series, 128), 0)
+    ids = jnp.zeros((n_series, 128), jnp.int32)
+    for s in range(n_series):
+        ids = jnp.where(series == s, ids_ref[s], ids)
+    member = (lax.broadcasted_iota(jnp.int32, (n_series, 128), 1) == ids).astype(F32)
+    magnitude = jnp.sum(jnp.abs(both[:n_series]), axis=1, keepdims=True)
+    counted = jnp.sum(obs, axis=1, keepdims=True)
+    own[...] = jnp.concatenate([
+        jnp.sum(member * magnitude, axis=0, keepdims=True), jnp.sum(member * counted, axis=0, keepdims=True),
+        jnp.zeros((6, 128), F32),
+    ], axis=0)
+
     lanes = lax.broadcasted_iota(jnp.int32, both.shape, 1)
 
     def one_lag(j, missing):
@@ -131,6 +156,10 @@
         feat_ref[s, nlag : nlag + 1, :] = jnp.ones((1, t), F32)
         feat_ref[s, nlag + 1 : nlag + 2, :] = missing[s : s + 1] * nlag**-0.5
         feat_ref[s, nlag + 2 :, :] = jnp.zeros((FPAD - nlag - 2, t), F32)
+
+    pl.semaphore_wait(barrier, parts - 1)
+    for c in copies:
+        c.start()
 
     w_in_rows = jnp.concatenate([in_ref[...].T, jnp.zeros((FPAD - nf, d), F32)], axis=0)
     w_in[...] = weight_cat(w_in_rows)
@@ -149,6 +178,15 @@
     gains[:, :1] = column(ga_ref[...])
     gains[:, 1:2] = column(gf_ref[...])
 
+    for c in copies:
+        c.wait()
+    total = own[...]
+    for i in range(parts - 1):
+        total = total + others[i]
+    set_scale = total[:1] / jnp.maximum(total[1:2], 1.0) + SCALE_EPS
+    series_scale = jnp.sum(jnp.where(member > 0.0, set_scale, 0.0), axis=1, keepdims=True)
+    scale_ref[...] = jnp.broadcast_to(series_scale, scale_ref.shape)
+
 
 def forward_kernel(
     scale_ref, feat_ref, w_in, w_qkv, w_out, w_gu, w_down, w_dh, w_dgu, w_dm, gains, cos_ref, sin_ref, cot_ref,
@@ -159,7 +197,7 @@
     d, t = cot_ref.shape[1], cot_ref.shape[2]
     ff = w_dh.shape[0]
     gain_attn, gain_ffn = gains[:, :1], gains[:, 1:2]
-    scales = row_scales(scale_ref[step], NLAG)
+    scales = row_scales(scale_ref[pl.ds(step, 1), :], NLAG)
 
     @pl.when(step == 0)
     def _():
@@ -483,7 +521,7 @@
             differentiate(items[j - AHEAD], *ahead.pop(j - AHEAD))
 
     gain = gains[:, :1]
-    scales = row_scales(scale_ref[step], NLAG)
+    scales = row_scales(scale_ref[pl.ds(step, 1), :], NLAG)
 
     def finish(i, _):
         cols = pl.ds(pl.multiple_of(i * TD, TD), TD)
@@ -572,9 +610,6 @@
     nf, d = in_proj.shape
     ff = gate_proj.shape[1]
     fs, ds = ff // parts, d // parts
-    onehot, sums = local_sums(series_values, observed, dataset_ids)
-    others = exchange_sums(sums, parts)
-
     cos, sin = rotation_tables(t)
     cos, sin = jnp.asarray(cos), jnp.asarray(sin)
     smem = pl.BlockSpec(memory_space=pltpu.SMEM)
@@ -592,11 +627,12 @@
     params = pltpu.CompilerParams(dimension_semantics=("arbitrary",), vmem_limit_bytes=62 * 2**20)
     plain = pltpu.CompilerParams(vmem_limit_bytes=62 * 2**20)
     in_t, down_t = in_proj.T, down_proj.T
-    raw, w_in, w_qkv, w_out, w_gu, w_down, w_dh, w_dgu, w_dm, w_dqkv, gains = pl.pallas_call(
-        prepare_kernel,
-        in_specs=[smem] * 2 + [vmem] * 12,
-        out_specs=[vmem] * 11,
+    series_scale, raw, w_in, w_qkv, w_out, w_gu, w_down, w_dh, w_dgu, w_dm, w_dqkv, gains = pl.pallas_call(
+        functools.partial(prepare_kernel, parts),
+        in_specs=[smem] * 3 + [vmem] * 12,
+        out_specs=[vmem] * 12,
         out_shape=[
+            shape(n_series, 128),
             shape(n_series, FPAD, t),
             shape(d, 3 * FPAD, dtype=BF16),
             shape(3 * d, 3 * d, dtype=BF16),
@@ -609,15 +645,16 @@
             shape(2 * d, 3 * d, dtype=BF16),
             shape(d, 128),
         ],
-        compiler_params=plain,
-        cost_estimate=pl.CostEstimate(flops=2 * 10**7, bytes_accessed=8 * 10**6, transcendentals=0),
-        name="split_weights_and_shift_lags",
-    )(lag_steps, lag_flags, series_values, observed, in_t, query_proj, key_proj, value_proj, out_proj, gate_proj, up_proj,
+        scratch_shapes=[
+            pltpu.VMEM((8, 128), F32),
+            pltpu.VMEM((parts - 1, 8, 128), F32),
+            pltpu.SemaphoreType.DMA((parts - 1,)),
+            pltpu.SemaphoreType.DMA((parts - 1,)),
+        ],
+        compiler_params=pltpu.CompilerParams(vmem_limit_bytes=62 * 2**20, collective_id=1, has_side_effects=True),
+        name="sums_weights_and_lags",
+    )(lag_steps, lag_flags, dataset_ids, series_values, observed, in_t, query_proj, key_proj, value_proj, out_proj, gate_proj, up_proj,
       down_t, gain_attn, gain_ffn)
-
-    sums = functools.reduce(jnp.add, others, sums)
-    set_scale = sums[0] / jnp.maximum(sums[1], 1.0) + SCALE_EPS
-    series_scale = jnp.sum(onehot * set_scale[None, :], axis=1)
 
     rows1 = round_up(round_up(3 * fs + ds + 1, 128) // 128 * d, 8 * groups)
     rows2 = round_up(round_up(3 * d + FPAD + 1, 128) // 128 * ds, 8 * groups)
@@ -626,7 +663,7 @@
     act, q, k, v, dm, st, da, x, b1 = pl.pallas_call(
         forward_kernel,
         grid=(n_series,),
-        in_specs=[smem, each(FPAD)] + [whole(a) for a in full] + [each(d)],
+        in_specs=[whole(series_scale), each(FPAD)] + [whole(a) for a in full] + [each(d)],
         out_specs=[each(d)] * 5 + [each(32)] + [each(d)] * 2 + [whole(b1)],
         out_shape=[shape(n_series, d, t)] * 5 + [shape(n_series, 32, t)] + [shape(n_series, d, t)] * 2 + [b1],
         scratch_shapes=[
@@ -660,7 +697,7 @@
     dx, total = pl.pallas_call(
         functools.partial(backward_kernel, n_series),
         grid=(n_series,),
-        in_specs=[smem] + [each(d)] * 4 + [each(32)] + [each(d)] * 2 + [each(FPAD)] + [whole(a) for a in full],
+        in_specs=[whole(series_scale)] + [each(d)] * 4 + [each(32)] + [each(d)] * 2 + [each(FPAD)] + [whole(a) for a in full],
         out_specs=[each(d), whole(total)],
         out_shape=[shape(n_series, d, t), total],
         scratch_shapes=[
@@ -698,18 +735,6 @@
         *grads[1:9],
         grads[9].T,
     )
-
-
-def local_sums(series_values, observed, dataset_ids):
-    observed_f = observed.astype(F32)
-    magnitude = jnp.sum(jnp.abs(series_values) * observed_f, axis=1)
-    counted = jnp.sum(observed_f, axis=1)
-    onehot = (dataset_ids[:, None] == jnp.arange(DSETS)[None, :]).astype(F32)
-    return onehot, jnp.sum(onehot[None] * jnp.stack([magnitude, counted])[:, :, None], axis=1)
-
-
-def exchange_sums(sums, parts):
-    return [lax.ppermute(sums, "narrow", [(i, (i + off) % parts) for i in range(parts)]) for off in range(1, parts)]
 
 
 def solution(mesh):

time: 169 us -> 166 us (0.982)
  Pallas kernels: 161 us -> 165 us
  starting transfers between devices: 3.24 us -> 0 us
  other arithmetic: 3.08 us -> 0 us
    pallas_call x2, Pallas kernels: 66 us -> 70.4 us  [the longest x1 60.3 us: on_device(): pl.pallas_call(forward_kernel, grid=(n_series,), in_specs=[whole(series_s...]
    ppermute x3 -> x0, starting transfers between devices: 3.24 us -> none  [exchange_sums(): lax.ppermute(sums, 'narrow', [(i, (i + off) % parts) for i in range(parts)])]
    reduce_sum x3 -> x0, other arithmetic: 2.32 us -> none  [the longest x1 1.35 us: on_device(): series_scale = jnp.sum(onehot * set_scale[None, :], axis=1)]
  transfers between devices with their start and end apart: 3 -> 0, of which waited for: 0 -> 0; matrix products, arithmetic and copies ran while one was open for 0% -> 0% of each run, Pallas kernels for 4% -> 0%
where the time goes in v3:
time: 166 us
  Pallas kernels  165 us (99%)
    pallas_call x1, Pallas kernels, on_device(): pl.pallas_call(functools.partial(backward_kernel, n_series), grid=(n_seri...  90 us
    pallas_call x1, Pallas kernels, on_device(): pl.pallas_call(forward_kernel, grid=(n_series,), in_specs=[whole(series_s...  60.3 us
    pallas_call x1, Pallas kernels, on_device(): pl.pallas_call(functools.partial(prepare_kernel, parts), in_specs=[smem]...  10.1 us
    pallas_call x1, Pallas kernels, on_device(): pl.pallas_call(unpack_kernel, grid=(n_series,), in_specs=[whole(total), e...  4.53 us

profile of v3, /device:TPU:0, one launch (start us, length us, event | category | flops | bytes accessed | tf_op | source)
XLA Modules:
  0.0 165.7 jit_solution(12081308360099897537)
XLA Ops:
  0.7 10.1 %sums_weights_and_lags.1 = (f32[4,128]{1,0:T(4,128)}, f32[4,96,1024]{2,1,0:T(8,128)}, bf16[144,288]{1,0:T(8,128)(2,1)}, bf16[432,432]{1,0:T(8,128)(2,1)}, bf16[1...) custom-call(s32[84]{0:T(128)} %lag_ref.1, ...), custom_call_target="tpu_custom_call" | custom-call | tf_op jit(solution)/shard_map/sums_weights_and_lags/pallas_call | solution.py:630
  10.7 60.3 %forward_and_ffn.1 = (f32[4,144,1024]{2,1,0:T(8,128)}, f32[4,144,1024]{2,1,0:T(8,128)}, f32[4,144,1024]{2,1,0:T(8,128)}, f32[4,144,1024]{2,1,0:T(8,128)}, f32[4,...) custom-call(f32[4,128]{1,0:T(4,128)} %get-tuple-element.46.scale_ref, ...), custom_call_target="tpu_custom_call" | custom-call | tf_op jit(solution)/shard_map/forward_and_ffn/pallas_call | solution.py:663
  71.0 90.0 %attention_backward_and_sums.1 = (f32[4,144,1024]{2,1,0:T(8,128)}, f32[8,80,128]{2,1,0:T(8,128)}) custom-call(f32[4,128]{1,0:T(4,128)} %get-tuple-element.46.scale_ref, f32[4,144,1024]{2,1,0:T(8,128)} %get-tuple-element.58.q_ref, f32[4,144,1024]{2,1,0:T(8,128)} %get-tuple-element.59.k_ref, f32[4,144,1024]{2,1,0:T(8,128)} %get-tuple-element.60.v_ref, ...), custom_call_target="tpu_custom_call" | custom-call | tf_op jit(solution)/shard_map/attention_backward_and_sums/pallas_call | solution.py:697
  161.0 4.5 %unpack_gradients.1 = (f32[4,144,1024]{2,1,0:T(8,128)}, f32[36,86]{1,0:T(8,128)}, f32[36]{0:T(128)}, f32[36,144]{1,0:T(8,128)}, f32[36,144]{1,0:T(8,128)}, /*ind...) custom-call(f32[8,80,128]{2,1,0:T(8,128)} %get-tuple-element.67.tota, ...), custom_call_target="tpu_custom_call" | custom-call | tf_op jit(solution)/shard_map/unpack_gradients/pallas_call | solution.py:722

commit v4 on v3

--- a/solution.py
+++ b/solution.py
@@ -108,15 +108,22 @@
 
 
 def prepare_kernel(
-    parts, lag_ref, flag_ref, ids_ref, vals_ref, obs_ref, in_ref, wq_ref, wk_ref, wv_ref, wo_ref, wg_ref, wu_ref, wd_ref,
-    ga_ref, gf_ref,
-    scale_ref, feat_ref, w_in, w_qkv, w_out, w_gu, w_down, w_dh, w_dgu, w_dm, w_dqkv, gains,
-    own, others, send_sem, recv_sem,
+    parts, n_in, lag_ref, flag_ref, ids_ref, *refs
 ):
+    sources, refs = refs[:n_in], refs[n_in:]
+    scale_ref, feat_ref, w_in, w_qkv, w_out, w_gu, w_down, w_dh, w_dgu, w_dm, w_dqkv, gains, cos_ref, sin_ref = refs[:14]
+    own, others, send_sem, recv_sem, fetch_sem, *fetched = refs[14:]
+    vals_ref, obs_ref, in_ref, wq_ref, wk_ref, wv_ref, wo_ref, wg_ref, wu_ref, wd_ref, ga_ref, gf_ref = fetched
+    fetched = fetched + [cos_ref, sin_ref]
+    fetches = [pltpu.make_async_copy(sources[i], fetched[i], fetch_sem.at[i]) for i in range(n_in)]
+    for c in fetches:
+        c.start()
     n_series, t = vals_ref.shape
     d, nf = in_ref.shape
     nlag = lag_ref.shape[0]
     ff = wg_ref.shape[1]
+    for c in fetches[:2]:
+        c.wait()
     obs = obs_ref[...].astype(F32)
     both = jnp.concatenate([vals_ref[...] * obs, obs], axis=0)
 
@@ -161,6 +168,8 @@
     for c in copies:
         c.start()
 
+    for c in fetches[2:]:
+        c.wait()
     w_in_rows = jnp.concatenate([in_ref[...].T, jnp.zeros((FPAD - nf, d), F32)], axis=0)
     w_in[...] = weight_cat(w_in_rows)
     for i, ref in enumerate((wq_ref, wk_ref, wv_ref)):
@@ -191,18 +200,27 @@
 def forward_kernel(
     scale_ref, feat_ref, w_in, w_qkv, w_out, w_gu, w_down, w_dh, w_dgu, w_dm, gains, cos_ref, sin_ref, cot_ref,
     act_ref, q_ref, k_ref, v_ref, dm_ref, st_ref, da_ref, x_ref, b1_ref,
-    mixed_ref, g_gu, g_down, g_out, g_gf,
+    mixed_ref, g_gu, g_down, g_out, g_gf, cot_buf, cot_sem,
 ):
     step = pl.program_id(0)
     d, t = cot_ref.shape[1], cot_ref.shape[2]
+
+    def fetch(i):
+        return pltpu.make_async_copy(cot_ref.at[i], cot_buf.at[i % 2], cot_sem.at[i % 2])
+
     ff = w_dh.shape[0]
     gain_attn, gain_ffn = gains[:, :1], gains[:, 1:2]
     scales = row_scales(scale_ref[pl.ds(step, 1), :], NLAG)
 
     @pl.when(step == 0)
     def _():
+        fetch(0).start()
         for ref in (g_gu, g_down, g_out, g_gf):
             ref[...] = jnp.zeros_like(ref)
+
+    @pl.when(step + 1 < pl.num_programs(0))
+    def _():
+        fetch(step + 1).start()
 
     st_ref[0] = jnp.zeros(st_ref.shape[1:], F32)
 
@@ -269,6 +287,8 @@
             item = items[j - AHEAD]
             mix(sides[item[0]], softmax(ahead.pop(j - AHEAD), item[1]), item)
 
+    fetch(step).wait()
+
     def feed(i, _):
         cols = pl.ds(pl.multiple_of(i * TC, TC), TC)
         mixed = mixed_ref[:, cols]
@@ -283,7 +303,7 @@
         hidden = silu * up
         act_ref[0, :, cols] = attended + mm_stack(w_down[...], hidden)
 
-        g = cot_ref[0, :, cols]
+        g = cot_buf[step % 2, :, cols]
         dh = nn(w_dh[...], cat3(g))
         dgate = dh * up * (sig + silu * (1.0 - sig))
         dup = dh * silu
@@ -598,6 +618,10 @@
     return np.cos(angles).astype(np.float32), np.sin(angles).astype(np.float32)
 
 
+def in_hbm(x):
+    return pltpu.with_memory_space_constraint(x, pltpu.HBM)
+
+
 def round_up(n, m):
     return (n + m - 1) // m * m
 
@@ -624,13 +648,16 @@
     def shape(*dims, dtype=F32):
         return jax.ShapeDtypeStruct(dims, dtype)
 
-    params = pltpu.CompilerParams(dimension_semantics=("arbitrary",), vmem_limit_bytes=62 * 2**20)
+    params = pltpu.CompilerParams(dimension_semantics=("arbitrary",), vmem_limit_bytes=28 * 2**20)
     plain = pltpu.CompilerParams(vmem_limit_bytes=62 * 2**20)
     in_t, down_t = in_proj.T, down_proj.T
-    series_scale, raw, w_in, w_qkv, w_out, w_gu, w_down, w_dh, w_dgu, w_dm, w_dqkv, gains = pl.pallas_call(
-        functools.partial(prepare_kernel, parts),
-        in_specs=[smem] * 3 + [vmem] * 12,
-        out_specs=[vmem] * 12,
+    hbm = pl.BlockSpec(memory_space=pltpu.HBM)
+    sources = [series_values, observed, in_t, query_proj, key_proj, value_proj, out_proj, gate_proj, up_proj, down_t,
+               gain_attn, gain_ffn, cos, sin]
+    series_scale, raw, w_in, w_qkv, w_out, w_gu, w_down, w_dh, w_dgu, w_dm, w_dqkv, gains, cos, sin = pl.pallas_call(
+        functools.partial(prepare_kernel, parts, len(sources)),
+        in_specs=[smem] * 3 + [hbm] * len(sources),
+        out_specs=[vmem] * 14,
         out_shape=[
             shape(n_series, 128),
             shape(n_series, FPAD, t),
@@ -644,17 +671,20 @@
             shape(d, 3 * d, dtype=BF16),
             shape(2 * d, 3 * d, dtype=BF16),
             shape(d, 128),
+            shape(*cos.shape),
+            shape(*sin.shape),
         ],
         scratch_shapes=[
             pltpu.VMEM((8, 128), F32),
             pltpu.VMEM((parts - 1, 8, 128), F32),
             pltpu.SemaphoreType.DMA((parts - 1,)),
             pltpu.SemaphoreType.DMA((parts - 1,)),
+            pltpu.SemaphoreType.DMA((len(sources),)),
+            *[pltpu.VMEM(a.shape, a.dtype) for a in sources[:12]],
         ],
-        compiler_params=pltpu.CompilerParams(vmem_limit_bytes=62 * 2**20, collective_id=1, has_side_effects=True),
+        compiler_params=pltpu.CompilerParams(vmem_limit_bytes=20 * 2**20, collective_id=1, has_side_effects=True),
         name="sums_weights_and_lags",
-    )(lag_steps, lag_flags, dataset_ids, series_values, observed, in_t, query_proj, key_proj, value_proj, out_proj, gate_proj, up_proj,
-      down_t, gain_attn, gain_ffn)
+    )(*[in_hbm(a) for a in (lag_steps, lag_flags, dataset_ids, *sources)])
 
     rows1 = round_up(round_up(3 * fs + ds + 1, 128) // 128 * d, 8 * groups)
     rows2 = round_up(round_up(3 * d + FPAD + 1, 128) // 128 * ds, 8 * groups)
@@ -663,7 +693,7 @@
     act, q, k, v, dm, st, da, x, b1 = pl.pallas_call(
         forward_kernel,
         grid=(n_series,),
-        in_specs=[whole(series_scale), each(FPAD)] + [whole(a) for a in full] + [each(d)],
+        in_specs=[whole(series_scale), each(FPAD)] + [whole(a) for a in full] + [hbm],
         out_specs=[each(d)] * 5 + [each(32)] + [each(d)] * 2 + [whole(b1)],
         out_shape=[shape(n_series, d, t)] * 5 + [shape(n_series, 32, t)] + [shape(n_series, d, t)] * 2 + [b1],
         scratch_shapes=[
@@ -672,10 +702,12 @@
             pltpu.VMEM((ff, d), F32),
             pltpu.VMEM((d, d), F32),
             pltpu.VMEM((d, 128), F32),
+            pltpu.VMEM((2, d, t), F32),
+            pltpu.SemaphoreType.DMA((2,)),
         ],
         compiler_params=params,
         name="forward_and_ffn",
-    )(series_scale, raw, *full, jnp.transpose(cotangent, (0, 2, 1)))
+    )(series_scale, raw, *full, in_hbm(jnp.transpose(cotangent, (0, 2, 1))))
 
     ny = parts // 2
     c1, c2 = rows1 // groups, rows2 // groups
@@ -710,7 +742,7 @@
             *buffers,
         ],
         compiler_params=pltpu.CompilerParams(
-            dimension_semantics=("arbitrary",), vmem_limit_bytes=62 * 2**20, collective_id=0, has_side_effects=True
+            dimension_semantics=("arbitrary",), vmem_limit_bytes=28 * 2**20, collective_id=0, has_side_effects=True
         ),
         name="attention_backward_and_sums",
     )(series_scale, q, k, v, dm, st, da, x, raw, *full)

time: 166 us -> 156 us (0.940)
  Pallas kernels: 165 us -> 155 us
    pallas_call x1, Pallas kernels: 90 us -> 86.3 us  [on_device(): pl.pallas_call(functools.partial(backward_kernel, n_series), grid=(n_seri...]
    pallas_call x1, Pallas kernels: 4.53 us -> 2.49 us  [on_device(): pl.pallas_call(unpack_kernel, grid=(n_series,), in_specs=[whole(total), e...]
    pallas_call x1, Pallas kernels: 60.3 us -> 58.3 us  [on_device(): pl.pallas_call(forward_kernel, grid=(n_series,), in_specs=[whole(series_s...]
    pallas_call x1, Pallas kernels: 10.1 us -> 8.15 us  [on_device(): pl.pallas_call(functools.partial(prepare_kernel, parts, len(sources)), in...]
where the time goes in v4:
time: 156 us
  Pallas kernels  155 us (99%)
    pallas_call x1, Pallas kernels, on_device(): pl.pallas_call(functools.partial(backward_kernel, n_series), grid=(n_seri...  86.3 us
    pallas_call x1, Pallas kernels, on_device(): pl.pallas_call(forward_kernel, grid=(n_series,), in_specs=[whole(series_s...  58.3 us
    pallas_call x1, Pallas kernels, on_device(): pl.pallas_call(functools.partial(prepare_kernel, parts, len(sources)), in...  8.15 us

profile of v4, /device:TPU:0, one launch (start us, length us, event | category | flops | bytes accessed | tf_op | source)
XLA Modules:
  0.0 156.0 jit_solution(8494040964504090504)
XLA Ops:
  0.7 8.1 %sums_weights_and_lags.1 = (f32[4,128]{1,0:T(4,128)S(1)}, f32[4,96,1024]{2,1,0:T(8,128)S(1)}, bf16[144,288]{1,0:T(8,128)(2,1)S(1)}, bf16[432,432]{1,0:T(8,128)(2...) custom-call(s32[84]{0:T(128)} %lag_ref.1, ...), custom_call_target="tpu_custom_call" | custom-call | tf_op jit(solution)/shard_map/sums_weights_and_lags/pallas_call | solution.py:657
  8.8 58.3 %forward_and_ffn.1 = (f32[4,144,1024]{2,1,0:T(8,128)}, f32[4,144,1024]{2,1,0:T(8,128)S(1)}, f32[4,144,1024]{2,1,0:T(8,128)S(1)}, f32[4,144,1024]{2,1,0:T(8,128)S...) custom-call(f32[4,128]{1,0:T(4,128)S(1)} %get-tuple-element.48.scale, ...), custom_call_target="tpu_custom_call" | custom-call | tf_op jit(solution)/shard_map/forward_and_ffn/pallas_call | solution.py:693
  67.1 86.3 %attention_backward_and_sums.1 = (f32[4,144,1024]{2,1,0:T(8,128)S(1)}, f32[8,80,128]{2,1,0:T(8,128)S(1)}) custom-call(f32[4,128]{1,0:T(4,128)S(1)} %get-tuple-element.48.scale_ref, f32[4,144,1024]{2,1,0:T(8,128)S(1)} %get-tuple-element.62.q_ref, f32[4,144,1024]{2,1,0:T(8,128)S(1)} %get-tuple-element.63.k_ref, f32[4,144,1024]{2,1,0:T(8,128)S(1)} %get-tuple-element.64.v_ref, ...), custom_call_target="tpu_custom_call" | custom-call | tf_op jit(solution)/shard_map/attention_backward_and_sums/pallas_call | solution.py:729
  153.3 2.5 %unpack_gradients.1 = (f32[4,144,1024]{2,1,0:T(8,128)}, f32[36,86]{1,0:T(8,128)}, f32[36]{0:T(128)}, f32[36,144]{1,0:T(8,128)}, f32[36,144]{1,0:T(8,128)}, /*ind...) custom-call(f32[8,80,128]{2,1,0:T(8,128)S(1)} %get-tuple-element.71., ...), custom_call_target="tpu_custom_call" | custom-call | tf_op jit(solution)/shard_map/unpack_gradients/pallas_call | solution.py:754

commit v5 on v4

--- a/solution.py
+++ b/solution.py
@@ -359,21 +359,26 @@
     return (group, narrow)
 
 
+def plane_peers(groups, ny):
+    g, n = lax.axis_index("group"), lax.axis_index("narrow")
+    core, y = lax.rem(n, 2), lax.div(n, 2)
+    for i in range(1, ny * groups):
+        peer_y, peer_g = lax.rem(y + i // groups, ny), lax.rem(g + i % groups, groups)
+        yield i, peer_y, peer_g, at(peer_g, peer_y * 2 + core)
+
+
 def greet(groups, ny):
     g, n = lax.axis_index("group"), lax.axis_index("narrow")
     core, y = lax.rem(n, 2), lax.div(n, 2)
     barrier = pltpu.get_barrier_semaphore()
-    peers = [at(g, y * 2 + 1 - core)]
-    peers += [at(g, lax.rem(y + off, ny) * 2 + core) for off in range(1, ny)]
-    peers += [at(lax.rem(g + off, groups), n) for off in range(1, groups)]
+    peers = [at(g, y * 2 + 1 - core)] + [peer for _, _, _, peer in plane_peers(groups, ny)]
     for peer in peers:
         pl.semaphore_signal(barrier, inc=1, device_id=peer, device_id_type=pl.DeviceIdType.MESH)
     pl.semaphore_wait(barrier, len(peers))
 
 
-def share_phases(src, total_ref, base, recv1, pair, recv2, share, recv3, send_sem, recv_sem):
-    ny, rows = src.shape[0], src.shape[2]
-    groups, chunk = recv3.shape[0], recv3.shape[1]
+def share_phases(src, total_ref, base, recv1, pair, recv2, send_sem, recv_sem):
+    ny, groups, chunk = pair.shape[:3]
     g, n = lax.axis_index("group"), lax.axis_index("narrow")
     core, y = lax.rem(n, 2), lax.div(n, 2)
 
@@ -386,18 +391,13 @@
     def over_core():
         return [copy(0, src.at[:, 1 - core], recv1, at(g, y * 2 + 1 - core))]
 
-    def over_y():
-        peers = [lax.rem(y + off, ny) for off in range(1, ny)]
-        return [copy(1 + i, pair.at[p], recv2.at[i], at(g, p * 2 + core)) for i, p in enumerate(peers)]
-
-    def over_group():
-        peers = [lax.rem(g + off, groups) for off in range(1, groups)]
-        return [copy(ny + i, share.at[p], recv3.at[1 + i], at(p, n)) for i, p in enumerate(peers)]
+    def over_plane():
+        return [copy(i, pair.at[py, pg], recv2.at[i], peer) for i, py, pg, peer in plane_peers(groups, ny)]
 
     def gather():
         own = total_ref.at[g, pl.ds(base, chunk)]
         peers = [lax.rem(g + off, groups) for off in range(1, groups)]
-        return [copy(ny + groups - 1 + i, own, own, at(p, n)) for i, p in enumerate(peers)]
+        return [copy(ny * groups + i, own, own, at(p, n)) for i, p in enumerate(peers)]
 
     def start(copies):
         for c in copies:
@@ -413,30 +413,22 @@
     def two():
         arrive(over_core())
         for i in range(ny):
-            pair[i] = src[i, core] + recv1[i]
-        start(over_y())
+            pair[i] = (src[i, core] + recv1[i]).reshape(groups, chunk, 128)
+        start(over_plane())
 
     def three():
-        arrive(over_y())
-        total = pair[y]
-        for i in range(ny - 1):
-            total += recv2[i]
-        share[...] = total.reshape(groups, chunk, 128)
-        start(over_group())
+        recv2[0] = pair[y, g]
+        arrive(over_plane())
+        total_ref[g, base : base + chunk] = jnp.sum(recv2[...], axis=0)
+        start(gather())
 
     def four():
-        recv3[0] = share[g]
-        arrive(over_group())
-        total_ref[g, base : base + chunk] = jnp.sum(recv3[...], axis=0)
-        start(gather())
-
-    def five():
         arrive(gather())
-        for copies in (over_core(), over_y(), over_group(), gather()):
+        for copies in (over_core(), over_plane(), gather()):
             for c in copies:
                 c.wait_send()
 
-    return one, two, three, four, five
+    return one, two, three, four
 
 
 def backward_kernel(
@@ -445,14 +437,14 @@
     dqkv_ref, g_qkv, g_in, g_ga, b2_ref, total_ref, *buffers,
 ):
     step = pl.program_id(0)
-    early = share_phases(b1_ref, total_ref, 0, *buffers[:7])
-    late = share_phases(b2_ref, total_ref, b1_ref.shape[2] // total_ref.shape[0], *buffers[7:])
+    early = share_phases(b1_ref, total_ref, 0, *buffers[:5])
+    late = share_phases(b2_ref, total_ref, b1_ref.shape[2] // total_ref.shape[0], *buffers[5:])
 
     @pl.when(step == 0)
     def _():
         greet(total_ref.shape[0], b1_ref.shape[0])
 
-    for i, phase in enumerate(early[:4]):
+    for i, phase in enumerate(early[:3]):
 
         @pl.when(step == min(i, dx_steps - 1))
         def _():
@@ -574,19 +566,21 @@
             own = slice(n * ds, (n + 1) * ds)
             share = jnp.concatenate([g_qkv_t[own], g_in[own, :], ga[own]], axis=1)
             b2_ref[n // 2, n % 2] = stack_columns(share, b2_ref.shape[2])
-        for phase in late[:4]:
+        for phase in late[:3]:
             phase()
-        for end in (early[4], late[4]):
+        for end in (early[3], late[3]):
             end()
         out_ref[...] = total_ref[...]
 
 
-def unpack_kernel(total_ref, dx_ref, dx_out, *grads):
-    dx_out[...] = dx_ref[...]
-
-    @pl.when(pl.program_id(0) == 0)
-    def _():
-        unpack(total_ref, *grads)
+def unpack_kernel(total_ref, dx_ref, dx_out, *refs):
+    grads, sems = refs[:-1], refs[-1]
+    copies = [pltpu.make_async_copy(dx_ref.at[i], dx_out.at[i], sems.at[i]) for i in range(dx_ref.shape[0])]
+    for c in copies:
+        c.start()
+    unpack(total_ref, *grads)
+    for c in copies:
+        c.wait()
 
 
 def unpack(total_ref, g_in, g_ga, g_q, g_k, g_v, g_out, g_gf, g_gate, g_up, g_down):
@@ -713,16 +707,14 @@
     c1, c2 = rows1 // groups, rows2 // groups
     total = shape(groups, c1 + c2, 128)
     full = [w_dqkv, gains, cos, sin, b1]
-    copies = ny + 2 * (groups - 1)
+    copies = ny * groups + groups - 1
     dma = pltpu.SemaphoreType.DMA
     buffers = []
     for rows, chunk in ((rows1, c1), (rows2, c2)):
         buffers += [
             pltpu.VMEM((ny, rows, 128), F32),
-            pltpu.VMEM((ny, rows, 128), F32),
-            pltpu.VMEM((max(ny - 1, 1), rows, 128), F32),
-            pltpu.VMEM((groups, chunk, 128), F32),
-            pltpu.VMEM((groups, chunk, 128), F32),
+            pltpu.VMEM((ny, groups, chunk, 128), F32),
+            pltpu.VMEM((ny * groups, chunk, 128), F32),
             dma((copies,)),
             dma((copies,)),
         ]
@@ -753,11 +745,11 @@
     ]
     dx, *grads = pl.pallas_call(
         unpack_kernel,
-        grid=(n_series,),
-        in_specs=[whole(total), each(d)],
-        out_specs=[each(d)] + [whole(a) for a in grads],
+        in_specs=[vmem, vmem],
+        out_specs=[hbm] + [vmem] * len(grads),
         out_shape=[shape(n_series, d, t)] + grads,
-        compiler_params=params,
+        scratch_shapes=[dma((n_series,))],
+        compiler_params=pltpu.CompilerParams(vmem_limit_bytes=28 * 2**20),
         name="unpack_gradients",
     )(total, dx)
     return (

time: 156 us -> 155 us (level)
  no operation moved by 1% of the time
where the time goes in v5:
time: 155 us
  Pallas kernels  154 us (99%)
    pallas_call x1, Pallas kernels, on_device(): pl.pallas_call(functools.partial(backward_kernel, n_series), grid=(n_seri...  85.8 us
    pallas_call x1, Pallas kernels, on_device(): pl.pallas_call(forward_kernel, grid=(n_series,), in_specs=[whole(series_s...  58.3 us
    pallas_call x1, Pallas kernels, on_device(): pl.pallas_call(functools.partial(prepare_kernel, parts, len(sources)), in...  8.15 us

profile of v5, /device:TPU:0, one launch (start us, length us, event | category | flops | bytes accessed | tf_op | source)
XLA Modules:
  0.0 155.2 jit_solution(6342241115193899029)
XLA Ops:
  0.7 8.1 %sums_weights_and_lags.1 = (f32[4,128]{1,0:T(4,128)S(1)}, f32[4,96,1024]{2,1,0:T(8,128)S(1)}, bf16[144,288]{1,0:T(8,128)(2,1)S(1)}, bf16[432,432]{1,0:T(8,128)(2...) custom-call(s32[84]{0:T(128)} %lag_ref.1, ...), custom_call_target="tpu_custom_call" | custom-call | tf_op jit(solution)/shard_map/sums_weights_and_lags/pallas_call | solution.py:651
  8.8 58.3 %forward_and_ffn.1 = (f32[4,144,1024]{2,1,0:T(8,128)}, f32[4,144,1024]{2,1,0:T(8,128)S(1)}, f32[4,144,1024]{2,1,0:T(8,128)S(1)}, f32[4,144,1024]{2,1,0:T(8,128)S...) custom-call(f32[4,128]{1,0:T(4,128)S(1)} %get-tuple-element.48.scale, ...), custom_call_target="tpu_custom_call" | custom-call | tf_op jit(solution)/shard_map/forward_and_ffn/pallas_call | solution.py:687
  67.1 85.8 %attention_backward_and_sums.1 = (f32[4,144,1024]{2,1,0:T(8,128)S(1)}, f32[8,80,128]{2,1,0:T(8,128)S(1)}) custom-call(f32[4,128]{1,0:T(4,128)S(1)} %get-tuple-element.48.scale_ref, f32[4,144,1024]{2,1,0:T(8,128)S(1)} %get-tuple-element.62.q_ref, f32[4,144,1024]{2,1,0:T(8,128)S(1)} %get-tuple-element.63.k_ref, f32[4,144,1024]{2,1,0:T(8,128)S(1)} %get-tuple-element.64.v_ref, ...), custom_call_target="tpu_custom_call" | custom-call | tf_op jit(solution)/shard_map/attention_backward_and_sums/pallas_call | solution.py:721
  152.9 2.2 %unpack_gradients.1 = (f32[4,144,1024]{2,1,0:T(8,128)}, f32[36,86]{1,0:T(8,128)}, f32[36]{0:T(128)}, f32[36,144]{1,0:T(8,128)}, f32[36,144]{1,0:T(8,128)}, /*ind...) custom-call(f32[8,80,128]{2,1,0:T(8,128)S(1)} %get-tuple-element.71., ...), custom_call_target="tpu_custom_call" | custom-call | tf_op jit(solution)/shard_map/unpack_gradients/pallas_call | solution.py:746
